TPU v7x, 32 devices: a whole 2x2x4 slice. The times are simulated.
32 devices in a mesh: dp: 8 (over z, y), seq: 4 (over x, core).
Axes of the slice: x: 2, y: 2, z: 4, core: 2. Of those that a mesh axis runs over, the one named last changes fastest.
Arguments:
- enc_input: bfloat16 [192, 98, 768], P(('dp', 'seq')), may hold values from -6 to 6
- keep_count: int32 [192], P(('dp', 'seq')), may hold values from 40 to 98, as said below
- keep_positions: int32 [192, 98], P(('dp', 'seq')), may hold values from 0 to 195, as said below
- enc_gain_one: bfloat16 [768], replicated, may hold values from 0.099609375 to 1.8984375
- enc_qkv_weight: bfloat16 [768, 2304], replicated, may hold values from -0.21875 to 0.21875
- enc_out_weight: bfloat16 [768, 768], replicated, may hold values from -0.625 to 0.625
- enc_gain_two: bfloat16 [768], replicated, may hold values from 0.099609375 to 1.8984375
- enc_up_weight: bfloat16 [768, 3072], replicated, may hold values from -0.21875 to 0.21875
- enc_down_weight: bfloat16 [3072, 768], replicated, may hold values from -0.15625 to 0.15625
- embed_weight: bfloat16 [768, 512], replicated, may hold values from -0.21875 to 0.21875
- mask_token: bfloat16 [512], replicated, may hold values from -4 to 4
- dec_gain_one: bfloat16 [512], replicated, may hold values from 0.099609375 to 1.8984375
- dec_qkv_weight: bfloat16 [512, 1536], replicated, may hold values from -0.25 to 0.25
- dec_out_weight: bfloat16 [512, 512], replicated, may hold values from -0.75 to 0.75
- dec_gain_two: bfloat16 [512], replicated, may hold values from 0.099609375 to 1.8984375
- dec_up_weight: bfloat16 [512, 2048], replicated, may hold values from -0.25 to 0.25
- dec_down_weight: bfloat16 [2048, 512], replicated, may hold values from -0.1875 to 0.1875
- cotangent: bfloat16 [192, 196, 512], P(('dp', 'seq')), may hold values from -6 to 6
Outputs:
- dec_output: bfloat16 [192, 196, 512], P(('dp', 'seq'))
- enc_input_grad: float32 [192, 98, 768], P(('dp', 'seq'))
- enc_gain_one_grad: float32 [768], P(('dp', 'seq'))
- enc_qkv_grad: float32 [768, 2304], P(('dp', 'seq'))
- enc_out_grad: float32 [768, 768], P(('dp', 'seq'))
- enc_gain_two_grad: float32 [768], P(('dp', 'seq'))
- enc_up_grad: float32 [768, 3072], P(('dp', 'seq'))
- enc_down_grad: float32 [3072, 768], P(('dp', 'seq'))
- embed_grad: float32 [768, 512], P(('dp', 'seq'))
- mask_token_grad: float32 [512], P(('dp', 'seq'))
- dec_gain_one_grad: float32 [512], P(('dp', 'seq'))
- dec_qkv_grad: float32 [512, 1536], P(('dp', 'seq'))
- dec_out_grad: float32 [512, 512], P(('dp', 'seq'))
- dec_gain_two_grad: float32 [512], P(('dp', 'seq'))
- dec_up_grad: float32 [512, 2048], P(('dp', 'seq'))
- dec_down_grad: float32 [2048, 512], P(('dp', 'seq'))
Inputs may be any that keep to these rules, and one draw needn't show every extreme that they name: `keep_count`: the number of visible patches of each image; some image has 98 and some image has 40. `keep_positions`: the entries of a row are distinct; the first keep_count entries are the image's visible patch positions, the others are unused.
All inputs are finite; a program needn't handle non-finite values.
Results may differ from a plain program's by a relative error of at most 0.02.
Values sent between devices are 32-bit elements; how exact they have to be, the bound alone decides.
A program may use at most 192 MiB of HBM per device.

v0:
```python
import math

import jax
import jax.numpy as jnp
from jax import lax
from jax.sharding import PartitionSpec as P

HEADS = 12
DHEADS = 16
PATCHES = 196


eps = 1e-06


def position_table(count, model_width):
    grid_side = math.isqrt(count)
    quarter = model_width // 4
    places = jnp.arange(count)
    across = (places % grid_side).astype(jnp.float32)
    row_place = (places // grid_side).astype(jnp.float32)
    frequency = 1.0 / 10000.0 ** (jnp.arange(quarter).astype(jnp.float32) / quarter)
    return jnp.concatenate(
        [
            jnp.sin(across[:, None] * frequency),
            jnp.cos(across[:, None] * frequency),
            jnp.sin(row_place[:, None] * frequency),
            jnp.cos(row_place[:, None] * frequency),
        ],
        axis=1,
    )


def contract(operand, matrix):
    return jnp.einsum("...i,ij->...j", operand, matrix, preferred_element_type=jnp.float32)


def contract_back(gradient, matrix):
    return jnp.einsum("...j,ij->...i", gradient, matrix, preferred_element_type=jnp.float32)


def outer_sum(operand, gradient):
    flat_left = operand.reshape(-1, operand.shape[-1])
    flat_right = gradient.reshape(-1, gradient.shape[-1])
    return lax.dot_general(
        flat_left, flat_right, (((0,), (0,)), ((), ())), preferred_element_type=jnp.float32
    )


def exact_gelu(values):
    return jax.nn.gelu(values, approximate=False)


def gelu_back(pre_act, grad_active):
    unused, pullback = jax.vjp(exact_gelu, pre_act)
    return pullback(grad_active)[0]


def layer_norm(stream, gain_vec):
    row_mean = jnp.mean(stream, axis=-1, keepdims=True)
    centered = stream - row_mean
    inverse = lax.rsqrt(jnp.mean(centered * centered, axis=-1, keepdims=True) + eps)
    unit_rows = centered * inverse
    return (unit_rows * gain_vec, unit_rows, inverse)


def layer_norm_back(grad_normed, unit_rows, inverse, gain_vec):
    grad_gain = jnp.sum((grad_normed * unit_rows).reshape(-1, unit_rows.shape[-1]), axis=0)
    grad_unit = grad_normed * gain_vec
    grad_stream = inverse * (
        grad_unit
        - jnp.mean(grad_unit, axis=-1, keepdims=True)
        - unit_rows * jnp.mean(grad_unit * unit_rows, axis=-1, keepdims=True)
    )
    return (grad_stream, grad_gain)


def attend(packed, head_count, key_mask):
    batch_size, row_count, triple_width = packed.shape
    model_width = triple_width // 3
    head_size = model_width // head_count
    queries = packed[:, :, :model_width].reshape(batch_size, row_count, head_count, head_size)
    key_heads = packed[:, :, model_width : 2 * model_width].reshape(
        batch_size, row_count, head_count, head_size
    )
    value_heads = packed[:, :, 2 * model_width :].reshape(
        batch_size, row_count, head_count, head_size
    )
    scores = jnp.einsum(
        "bqhd,bkhd->bhqk", queries, key_heads, preferred_element_type=jnp.float32
    ) * head_size ** (-0.5)
    if key_mask is not None:
        scores = jnp.where(key_mask[:, None, None, :], scores, -1e30)
    row_max = jnp.max(scores, axis=-1, keepdims=True)
    raised = jnp.exp(scores - row_max)
    attn_weights = raised / jnp.sum(raised, axis=-1, keepdims=True)
    attn_low = attn_weights.astype(jnp.bfloat16)
    mixed_heads = jnp.einsum(
        "bhqk,bkhd->bqhd", attn_low, value_heads, preferred_element_type=jnp.float32
    )
    mixed_heads = mixed_heads.reshape(batch_size, row_count, model_width).astype(jnp.bfloat16)
    return (mixed_heads, attn_weights, attn_low)


def attend_back(packed, attn_weights, attn_low, grad_mixed, head_count):
    batch_size, row_count, triple_width = packed.shape
    model_width = triple_width // 3
    head_size = model_width // head_count
    factor = head_size ** (-0.5)
    queries = packed[:, :, :model_width].reshape(batch_size, row_count, head_count, head_size)
    key_heads = packed[:, :, model_width : 2 * model_width].reshape(
        batch_size, row_count, head_count, head_size
    )
    value_heads = packed[:, :, 2 * model_width :].reshape(
        batch_size, row_count, head_count, head_size
    )
    grad_heads = grad_mixed.reshape(batch_size, row_count, head_count, head_size)
    grad_values = jnp.einsum(
        "bhqk,bqhd->bkhd", attn_low, grad_heads, preferred_element_type=jnp.float32
    )
    grad_attn = jnp.einsum(
        "bqhd,bkhd->bhqk", grad_heads, value_heads, preferred_element_type=jnp.float32
    )
    grad_scores = attn_weights * (
        grad_attn - jnp.sum(attn_weights * grad_attn, axis=-1, keepdims=True)
    )
    grad_scores = grad_scores.astype(jnp.bfloat16)
    grad_queries = (
        jnp.einsum("bhqk,bkhd->bqhd", grad_scores, key_heads, preferred_element_type=jnp.float32)
        * factor
    )
    grad_keys = (
        jnp.einsum("bhqk,bqhd->bkhd", grad_scores, queries, preferred_element_type=jnp.float32)
        * factor
    )
    grad_packed = jnp.concatenate(
        [
            grad_queries.reshape(batch_size, row_count, model_width),
            grad_keys.reshape(batch_size, row_count, model_width),
            grad_values.reshape(batch_size, row_count, model_width),
        ],
        axis=-1,
    )
    return grad_packed.astype(jnp.bfloat16)


def mlp_forward(middle, gain_two, up_weight, down_weight):
    normed_two, unit_two, inverse_two = layer_norm(middle, gain_two.astype(jnp.float32))
    second_low = normed_two.astype(jnp.bfloat16)
    pre_act = contract(second_low, up_weight)
    active_low = exact_gelu(pre_act).astype(jnp.bfloat16)
    result = middle + contract(active_low, down_weight)
    return (
        result,
        {
            "unit_two": unit_two,
            "inverse_two": inverse_two,
            "second_low": second_low,
            "pre_act": pre_act,
            "active_low": active_low,
        },
    )


def mlp_backward(grad_result, kept_values, gain_two, up_weight, down_weight):
    grad_branch = grad_result.astype(jnp.bfloat16)
    grad_down = outer_sum(kept_values["active_low"], grad_branch)
    grad_active = contract_back(grad_branch, down_weight)
    grad_pre = gelu_back(kept_values["pre_act"], grad_active).astype(jnp.bfloat16)
    grad_up = outer_sum(kept_values["second_low"], grad_pre)
    grad_second = contract_back(grad_pre, up_weight)
    grad_middle, grad_gain_two = layer_norm_back(
        grad_second,
        kept_values["unit_two"],
        kept_values["inverse_two"],
        gain_two.astype(jnp.float32),
    )
    return (grad_middle + grad_result, grad_gain_two, grad_up, grad_down)


def block_forward(stream, weights, head_count, key_mask):
    gain_one, qkv_weight, out_weight, gain_two, up_weight, down_weight = weights
    normed_one, unit_one, inverse_one = layer_norm(stream, gain_one.astype(jnp.float32))
    normed_low = normed_one.astype(jnp.bfloat16)
    packed = contract(normed_low, qkv_weight).astype(jnp.bfloat16)
    mixed_heads, attn_weights, attn_low = attend(packed, head_count, key_mask)
    middle = stream + contract(mixed_heads, out_weight)
    result, mlp_kept = mlp_forward(middle, gain_two, up_weight, down_weight)
    kept_values = {
        "unit_one": unit_one,
        "inverse_one": inverse_one,
        "normed_low": normed_low,
        "packed": packed,
        "attn_weights": attn_weights,
        "attn_low": attn_low,
        "mixed_heads": mixed_heads,
        "mlp": mlp_kept,
    }
    return (result, kept_values)


def block_backward(grad_result, kept_values, weights, head_count):
    gain_one, qkv_weight, out_weight, gain_two, up_weight, down_weight = weights
    grad_middle, grad_gain_two, grad_up, grad_down = mlp_backward(
        grad_result, kept_values["mlp"], gain_two, up_weight, down_weight
    )
    grad_attend = grad_middle.astype(jnp.bfloat16)
    grad_out = outer_sum(kept_values["mixed_heads"], grad_attend)
    grad_mixed = contract_back(grad_attend, out_weight).astype(jnp.bfloat16)
    grad_packed = attend_back(
        kept_values["packed"],
        kept_values["attn_weights"],
        kept_values["attn_low"],
        grad_mixed,
        head_count,
    )
    grad_qkv = outer_sum(kept_values["normed_low"], grad_packed)
    grad_normed = contract_back(grad_packed, qkv_weight)
    grad_stream, grad_gain_one = layer_norm_back(
        grad_normed,
        kept_values["unit_one"],
        kept_values["inverse_one"],
        gain_one.astype(jnp.float32),
    )
    return (
        grad_stream + grad_middle,
        grad_gain_one,
        grad_qkv,
        grad_out,
        grad_gain_two,
        grad_up,
        grad_down,
    )


def micro_step(
    enc_rows, counts, positions, cot_rows, enc_weights, embed_weight, mask_token, dec_weights
):
    slot_total = enc_rows.shape[1]
    live_slots = jnp.arange(slot_total)[None, :] < counts[:, None]
    encoded, enc_kept = block_forward(enc_rows.astype(jnp.float32), enc_weights, HEADS, live_slots)
    encoded_low = encoded.astype(jnp.bfloat16)
    embedded = contract(encoded_low, embed_weight)
    places = jnp.arange(PATCHES)
    matches = (positions[:, :, None] == places[None, None, :]) & live_slots[:, :, None]
    covered = jnp.any(matches, axis=1)
    slot_index = jnp.sum(jnp.where(matches, jnp.arange(slot_total)[None, :, None], 0), axis=1)
    picked = jnp.take_along_axis(embedded, slot_index[:, :, None], axis=1)
    filled = jnp.where(covered[:, :, None], picked, mask_token.astype(jnp.float32))
    filled = filled + position_table(PATCHES, embedded.shape[-1])
    filled_low = filled.astype(jnp.bfloat16)
    decoded, dec_kept = block_forward(filled_low.astype(jnp.float32), dec_weights, DHEADS, None)
    dec_piece = decoded.astype(jnp.bfloat16)
    dec_back = block_backward(cot_rows.astype(jnp.float32), dec_kept, dec_weights, DHEADS)
    dec_terms = dec_back[1:]
    grad_filled = dec_back[0].astype(jnp.bfloat16).astype(jnp.float32)
    mask_term = jnp.sum(
        jnp.where(covered[:, :, None], 0.0, grad_filled).reshape(-1, grad_filled.shape[-1]), axis=0
    )
    grad_embedded = jnp.take_along_axis(grad_filled, positions[:, :, None], axis=1)
    grad_embedded = jnp.where(live_slots[:, :, None], grad_embedded, 0.0).astype(jnp.bfloat16)
    embed_term = outer_sum(encoded_low, grad_embedded)
    grad_encoded = contract_back(grad_embedded, embed_weight)
    enc_back = block_backward(grad_encoded, enc_kept, enc_weights, HEADS)
    grad_input = enc_back[0]
    enc_terms = enc_back[1:] + (embed_term, mask_term)
    return (dec_piece, grad_input, tuple(enc_terms) + tuple(dec_terms))


def local(
    enc_input,
    keep_count,
    keep_positions,
    enc_gain_one,
    enc_qkv_weight,
    enc_out_weight,
    enc_gain_two,
    enc_up_weight,
    enc_down_weight,
    embed_weight,
    mask_token,
    dec_gain_one,
    dec_qkv_weight,
    dec_out_weight,
    dec_gain_two,
    dec_up_weight,
    dec_down_weight,
    cotangent,
):
    enc_weights = (
        enc_gain_one,
        enc_qkv_weight,
        enc_out_weight,
        enc_gain_two,
        enc_up_weight,
        enc_down_weight,
    )
    dec_weights = (
        dec_gain_one,
        dec_qkv_weight,
        dec_out_weight,
        dec_gain_two,
        dec_up_weight,
        dec_down_weight,
    )
    all_params = (
        enc_gain_one,
        enc_qkv_weight,
        enc_out_weight,
        enc_gain_two,
        enc_up_weight,
        enc_down_weight,
        embed_weight,
        mask_token,
        dec_gain_one,
        dec_qkv_weight,
        dec_out_weight,
        dec_gain_two,
        dec_up_weight,
        dec_down_weight,
    )
    totals = tuple((jnp.zeros(param.shape, jnp.float32) for param in all_params))

    def one_micro(running, pieces):
        enc_rows, counts, positions, cot_rows = pieces
        dec_piece, grad_input, terms = micro_step(
            enc_rows,
            counts,
            positions,
            cot_rows,
            enc_weights,
            embed_weight,
            mask_token,
            dec_weights,
        )
        running = tuple((total + term for total, term in zip(running, terms)))
        return (running, (dec_piece, grad_input))

    totals, (dec_pieces, input_grads) = lax.scan(
        one_micro,
        totals,
        (enc_input[:, None], keep_count[:, None], keep_positions[:, None], cotangent[:, None]),
    )
    totals = (
        lax.psum_scatter(totals[0], ("dp", "seq"), scatter_dimension=0, tiled=True),
        lax.psum_scatter(totals[1], ("dp", "seq"), scatter_dimension=0, tiled=True),
        lax.psum_scatter(totals[2], ("dp", "seq"), scatter_dimension=0, tiled=True),
        lax.psum_scatter(totals[3], ("dp", "seq"), scatter_dimension=0, tiled=True),
        lax.psum_scatter(totals[4], ("dp", "seq"), scatter_dimension=0, tiled=True),
        lax.psum_scatter(totals[5], ("dp", "seq"), scatter_dimension=0, tiled=True),
        lax.psum_scatter(totals[6], ("dp", "seq"), scatter_dimension=0, tiled=True),
        lax.psum_scatter(totals[7], ("dp", "seq"), scatter_dimension=0, tiled=True),
        lax.psum_scatter(totals[8], ("dp", "seq"), scatter_dimension=0, tiled=True),
        lax.psum_scatter(totals[9], ("dp", "seq"), scatter_dimension=0, tiled=True),
        lax.psum_scatter(totals[10], ("dp", "seq"), scatter_dimension=0, tiled=True),
        lax.psum_scatter(totals[11], ("dp", "seq"), scatter_dimension=0, tiled=True),
        lax.psum_scatter(totals[12], ("dp", "seq"), scatter_dimension=0, tiled=True),
        lax.psum_scatter(totals[13], ("dp", "seq"), scatter_dimension=0, tiled=True),
    )
    dec_output = dec_pieces.reshape(cotangent.shape)
    enc_input_grad = input_grads.reshape(enc_input.shape)
    return (
        dec_output,
        enc_input_grad,
        totals[0],
        totals[1],
        totals[2],
        totals[3],
        totals[4],
        totals[5],
        totals[6],
        totals[7],
        totals[8],
        totals[9],
        totals[10],
        totals[11],
        totals[12],
        totals[13],
    )


def solution(mesh):
    placed = (
        P(("dp", "seq"), None, None),
        P(("dp", "seq")),
        P(("dp", "seq"), None),
        P(),
        P(),
        P(),
        P(),
        P(),
        P(),
        P(),
        P(),
        P(),
        P(),
        P(),
        P(),
        P(),
        P(),
        P(("dp", "seq"), None, None),
    )
    return jax.shard_map(
        local,
        mesh=mesh,
        in_specs=placed,
        out_specs=(
            P(("dp", "seq"), None, None),
            P(("dp", "seq"), None, None),
            P(("dp", "seq")),
            P(("dp", "seq"), None),
            P(("dp", "seq"), None),
            P(("dp", "seq")),
            P(("dp", "seq"), None),
            P(("dp", "seq"), None),
            P(("dp", "seq"), None),
            P(("dp", "seq")),
            P(("dp", "seq")),
            P(("dp", "seq"), None),
            P(("dp", "seq"), None),
            P(("dp", "seq")),
            P(("dp", "seq"), None),
            P(("dp", "seq"), None),
        ),
        check_vma=False,
    )
```

profile of v0, /device:TPU:0, one launch (start us, length us, event | category | flops | bytes accessed | tf_op | source)
XLA Modules:
  0.0 1849.6 jit_solution(4033830428015421300)
XLA Ops:
  8.1 702.7 %while.43 = (s32[]{:T(128)}, f32[768]{0:T(1024)}, f32[768,2304]{1,0:T(8,128)}, f32[768,768]{1,0:T(8,128)}, f32[768]{0:T(1024)}, /*index=5*/f32[768,3072]{1,0:T(8...) while((s32[]{:T(128)}, f32[768]{0:T(1024)}, ...), condition=%wide.region_30.31_spmd.clone, body=%wide.region_0.30_spmd.clone.sunk | while | flops 8593786880 | bytes 487885344 | solution.py:339
  23.5 5.8 fusion.362
  61.8 6.6 add_convert_fusion.5
  94.8 6.0 select_add_fusion.26
  132.7 6.0 fusion.362
  171.1 6.6 add_convert_fusion.5
  206.8 6.0 select_add_fusion.26
  212.9 10.7 select_add_fusion.23
  289.5 6.6 add_convert_fusion.5
  325.3 6.0 select_add_fusion.26
  331.4 10.7 select_add_fusion.23
  369.4 6.0 fusion.362
  407.7 6.6 add_convert_fusion.5
  443.5 6.0 select_add_fusion.26
  449.6 10.7 select_add_fusion.23
  526.2 6.6 add_convert_fusion.5
  561.9 6.0 select_add_fusion.26
  568.0 10.7 select_add_fusion.23
  606.0 6.0 fusion.362
  644.4 6.6 add_convert_fusion.5
  680.2 6.0 select_add_fusion.26
  686.3 10.7 select_add_fusion.23
  716.3 42.2 %all-reduce.5 = (f32[768]{0:T(1024)S(1)}, f32[768]{0:T(1024)S(1)}, f32[512]{0:T(512)S(1)}, f32[512]{0:T(512)S(1)}, f32[512]{0:T(512)S(1)}) all-reduce(f32[768]{0:T(1024)S(1)} %copy-done.64, f32[768]{0:T(1024)S(1)} %copy-done.67, f32[512]{0:T(512)S(1)} %copy-done.85, ...), channel_id=2, replica_groups=mesh['dp'=8,'seq'=4] {'dp','seq'}, use_global_device_ids=true, to_apply=%region_31.32.clone | all-reduce | flops 3072 | bytes 24576
  761.4 49.1 %reduce-scatter.18.cloned.1.call-done = f32[24,512]{1,0:T(8,128)} async-done(((f32[768,512]{1,0:T(8,128)}), f32[24,512]{1,0:T(8,128)}) %reduce-scatter.18.cloned.1.call-update) | async-done | bytes 49168 | tf_op jit(solution)/shard_map/reduce_scatter | solution.py:351
  810.6 137.1 %reduce-scatter.22.cloned.1.call-done = f32[16,512]{1,0:T(8,128)} async-done(((f32[512,512]{1,0:T(8,128)}), f32[16,512]{1,0:T(8,128)}) %reduce-scatter.22.cloned.1.call-update) | async-done | bytes 32784 | tf_op jit(solution)/shard_map/reduce_scatter | solution.py:355
  947.7 101.7 %reduce-scatter.12.cloned.1.call-done = f32[24,768]{1,0:T(8,128)} async-done(((f32[768,768]{1,0:T(8,128)}), f32[24,768]{1,0:T(8,128)}) %reduce-scatter.12.cloned.1.call-update) | async-done | bytes 73744 | tf_op jit(solution)/shard_map/reduce_scatter | solution.py:347
  1049.4 106.4 %reduce-scatter.20.cloned.1.call-done = f32[16,1536]{1,0:T(8,128)} async-done(((f32[512,1536]{1,0:T(8,128)}), f32[16,1536]{1,0:T(8,128)}) %reduce-scatter.20.cloned.1.call-update) | async-done | bytes 98320 | tf_op jit(solution)/shard_map/reduce_scatter | solution.py:354
  1155.8 142.3 %reduce-scatter.24.cloned.1.call-done = f32[16,2048]{1,0:T(8,128)} async-done(((f32[512,2048]{1,0:T(8,128)}), f32[16,2048]{1,0:T(8,128)}) %reduce-scatter.24.cloned.1.call-update) | async-done | bytes 131088 | tf_op jit(solution)/shard_map/reduce_scatter | solution.py:357
  1298.1 139.7 %reduce-scatter.26.cloned.1.call-done = f32[64,512]{1,0:T(8,128)} async-done(((f32[2048,512]{1,0:T(8,128)}), f32[64,512]{1,0:T(8,128)}) %reduce-scatter.26.cloned.1.call-update) | async-done | bytes 131088 | tf_op jit(solution)/shard_map/reduce_scatter | solution.py:358
  1437.8 121.5 %reduce-scatter.10.cloned.1.call-done = f32[24,2304]{1,0:T(8,128)} async-done(((f32[768,2304]{1,0:T(8,128)}), f32[24,2304]{1,0:T(8,128)}) %reduce-scatter.10.cloned.1.call-update) | async-done | bytes 221200 | tf_op jit(solution)/shard_map/reduce_scatter | solution.py:346
  1559.3 142.4 %reduce-scatter.14.cloned.1.call-done = f32[24,3072]{1,0:T(8,128)} async-done(((f32[768,3072]{1,0:T(8,128)}), f32[24,3072]{1,0:T(8,128)}) %reduce-scatter.14.cloned.1.call-update) | async-done | bytes 294928 | tf_op jit(solution)/shard_map/reduce_scatter | solution.py:349
  1701.6 141.1 %reduce-scatter.16.cloned.1.call-done = f32[96,768]{1,0:T(8,128)} async-done(((f32[3072,768]{1,0:T(8,128)}), f32[96,768]{1,0:T(8,128)}) %reduce-scatter.16.cloned.1.call-update) | async-done | bytes 294928 | tf_op jit(solution)/shard_map/reduce_scatter | solution.py:350
  (1865 shorter events, 546.4 us)
Async XLA Ops:
  7.2 803.4 %reduce-scatter.18.cloned.1.call-start = ((), (), s32[]{:S(2)}) async-start(), calls=%async_computation.13 | async-start | bytes 1622016 | tf_op jit(solution)/shard_map/reduce_scatter | solution.py:351
  8.1 52.3 %copy-start.92 = (s32[6,1,98]{2,1,0:T(1,128)}, s32[6,1,98]{2,1,0:T(1,128)S(1)}, u32[]{:S(2)}) copy-start(s32[6,1,98]{2,1,0:T(1,128)S(1)} %get-tuple-element.1144) | copy-start | bytes 7060 | tf_op jit(solution)/shard_map/while
  15.7 45.5 %copy-start.71 = (pred[98]{0:T(512)(128)(4,1)}, pred[98]{0:T(512)(128)(4,1)S(1)}, u32[]{:S(2)}) copy-start(pred[98]{0:T(512)(128)(4,1)S(1)} %iota_compare_fusion.2) | copy-start | bytes 298 | tf_op jit(solution)/shard_map/while
  20.0 50.8 %copy-start.50 = (f32[98]{0:T(128)}, f32[98]{0:T(128)S(1)}, u32[]{:S(2)}) copy-start(f32[98]{0:T(128)S(1)} %broadcast_multiply_fusion.24) | copy-start | bytes 1180 | tf_op jit(solution)/shard_map/while
  20.2 48.3 %copy-start.54 = (f32[98]{0:T(128)}, f32[98]{0:T(128)S(1)}, u32[]{:S(2)}) copy-start(f32[98]{0:T(128)S(1)} %add_rsqrt_fusion.9) | copy-start | bytes 1180 | tf_op jit(solution)/shard_map/while
  117.3 52.3 %copy-start.92 = (s32[6,1,98]{2,1,0:T(1,128)}, s32[6,1,98]{2,1,0:T(1,128)S(1)}, u32[]{:S(2)}) copy-start(s32[6,1,98]{2,1,0:T(1,128)S(1)} %get-tuple-element.1144) | copy-start | bytes 7060 | tf_op jit(solution)/shard_map/while
  125.0 45.5 %copy-start.71 = (pred[98]{0:T(512)(128)(4,1)}, pred[98]{0:T(512)(128)(4,1)S(1)}, u32[]{:S(2)}) copy-start(pred[98]{0:T(512)(128)(4,1)S(1)} %iota_compare_fusion.2) | copy-start | bytes 298 | tf_op jit(solution)/shard_map/while
  129.2 50.8 %copy-start.50 = (f32[98]{0:T(128)}, f32[98]{0:T(128)S(1)}, u32[]{:S(2)}) copy-start(f32[98]{0:T(128)S(1)} %broadcast_multiply_fusion.24) | copy-start | bytes 1180 | tf_op jit(solution)/shard_map/while
  129.4 48.3 %copy-start.54 = (f32[98]{0:T(128)}, f32[98]{0:T(128)S(1)}, u32[]{:S(2)}) copy-start(f32[98]{0:T(128)S(1)} %add_rsqrt_fusion.9) | copy-start | bytes 1180 | tf_op jit(solution)/shard_map/while
  235.8 52.3 %copy-start.92 = (s32[6,1,98]{2,1,0:T(1,128)}, s32[6,1,98]{2,1,0:T(1,128)S(1)}, u32[]{:S(2)}) copy-start(s32[6,1,98]{2,1,0:T(1,128)S(1)} %get-tuple-element.1144) | copy-start | bytes 7060 | tf_op jit(solution)/shard_map/while
  243.4 45.5 %copy-start.71 = (pred[98]{0:T(512)(128)(4,1)}, pred[98]{0:T(512)(128)(4,1)S(1)}, u32[]{:S(2)}) copy-start(pred[98]{0:T(512)(128)(4,1)S(1)} %iota_compare_fusion.2) | copy-start | bytes 298 | tf_op jit(solution)/shard_map/while
  247.6 50.8 %copy-start.50 = (f32[98]{0:T(128)}, f32[98]{0:T(128)S(1)}, u32[]{:S(2)}) copy-start(f32[98]{0:T(128)S(1)} %broadcast_multiply_fusion.24) | copy-start | bytes 1180 | tf_op jit(solution)/shard_map/while
  247.9 48.3 %copy-start.54 = (f32[98]{0:T(128)}, f32[98]{0:T(128)S(1)}, u32[]{:S(2)}) copy-start(f32[98]{0:T(128)S(1)} %add_rsqrt_fusion.9) | copy-start | bytes 1180 | tf_op jit(solution)/shard_map/while
  354.0 52.3 %copy-start.92 = (s32[6,1,98]{2,1,0:T(1,128)}, s32[6,1,98]{2,1,0:T(1,128)S(1)}, u32[]{:S(2)}) copy-start(s32[6,1,98]{2,1,0:T(1,128)S(1)} %get-tuple-element.1144) | copy-start | bytes 7060 | tf_op jit(solution)/shard_map/while
  361.6 45.5 %copy-start.71 = (pred[98]{0:T(512)(128)(4,1)}, pred[98]{0:T(512)(128)(4,1)S(1)}, u32[]{:S(2)}) copy-start(pred[98]{0:T(512)(128)(4,1)S(1)} %iota_compare_fusion.2) | copy-start | bytes 298 | tf_op jit(solution)/shard_map/while
  365.9 50.8 %copy-start.50 = (f32[98]{0:T(128)}, f32[98]{0:T(128)S(1)}, u32[]{:S(2)}) copy-start(f32[98]{0:T(128)S(1)} %broadcast_multiply_fusion.24) | copy-start | bytes 1180 | tf_op jit(solution)/shard_map/while
  366.1 48.3 %copy-start.54 = (f32[98]{0:T(128)}, f32[98]{0:T(128)S(1)}, u32[]{:S(2)}) copy-start(f32[98]{0:T(128)S(1)} %add_rsqrt_fusion.9) | copy-start | bytes 1180 | tf_op jit(solution)/shard_map/while
  472.4 52.3 %copy-start.92 = (s32[6,1,98]{2,1,0:T(1,128)}, s32[6,1,98]{2,1,0:T(1,128)S(1)}, u32[]{:S(2)}) copy-start(s32[6,1,98]{2,1,0:T(1,128)S(1)} %get-tuple-element.1144) | copy-start | bytes 7060 | tf_op jit(solution)/shard_map/while
  480.1 45.5 %copy-start.71 = (pred[98]{0:T(512)(128)(4,1)}, pred[98]{0:T(512)(128)(4,1)S(1)}, u32[]{:S(2)}) copy-start(pred[98]{0:T(512)(128)(4,1)S(1)} %iota_compare_fusion.2) | copy-start | bytes 298 | tf_op jit(solution)/shard_map/while
  484.3 50.8 %copy-start.50 = (f32[98]{0:T(128)}, f32[98]{0:T(128)S(1)}, u32[]{:S(2)}) copy-start(f32[98]{0:T(128)S(1)} %broadcast_multiply_fusion.24) | copy-start | bytes 1180 | tf_op jit(solution)/shard_map/while
  484.5 48.3 %copy-start.54 = (f32[98]{0:T(128)}, f32[98]{0:T(128)S(1)}, u32[]{:S(2)}) copy-start(f32[98]{0:T(128)S(1)} %add_rsqrt_fusion.9) | copy-start | bytes 1180 | tf_op jit(solution)/shard_map/while
  590.6 52.3 %copy-start.92 = (s32[6,1,98]{2,1,0:T(1,128)}, s32[6,1,98]{2,1,0:T(1,128)S(1)}, u32[]{:S(2)}) copy-start(s32[6,1,98]{2,1,0:T(1,128)S(1)} %get-tuple-element.1144) | copy-start | bytes 7060 | tf_op jit(solution)/shard_map/while
  602.5 50.8 %copy-start.50 = (f32[98]{0:T(128)}, f32[98]{0:T(128)S(1)}, u32[]{:S(2)}) copy-start(f32[98]{0:T(128)S(1)} %broadcast_multiply_fusion.24) | copy-start | bytes 1180 | tf_op jit(solution)/shard_map/while
  602.7 48.3 %copy-start.54 = (f32[98]{0:T(128)}, f32[98]{0:T(128)S(1)}, u32[]{:S(2)}) copy-start(f32[98]{0:T(128)S(1)} %add_rsqrt_fusion.9) | copy-start | bytes 1180 | tf_op jit(solution)/shard_map/while
  710.8 236.9 %reduce-scatter.22.cloned.1.call-start = ((), (), s32[]{:S(2)}) async-start(), calls=%async_computation.15 | async-start | bytes 1081344 | tf_op jit(solution)/shard_map/reduce_scatter | solution.py:355
  711.5 337.9 %reduce-scatter.12.cloned.1.call-start = ((), (), s32[]{:S(2)}) async-start(), calls=%async_computation.10 | async-start | bytes 2433024 | tf_op jit(solution)/shard_map/reduce_scatter | solution.py:347
  712.3 443.6 %reduce-scatter.20.cloned.1.call-start = ((), (), s32[]{:S(2)}) async-start(), calls=%async_computation.14 | async-start | bytes 3244032 | tf_op jit(solution)/shard_map/reduce_scatter | solution.py:354
  712.8 585.3 %reduce-scatter.24.cloned.1.call-start = ((), (), s32[]{:S(2)}) async-start(), calls=%async_computation.16 | async-start | bytes 4325376 | tf_op jit(solution)/shard_map/reduce_scatter | solution.py:357
  713.4 724.4 %reduce-scatter.26.cloned.1.call-start = ((), (), s32[]{:S(2)}) async-start(), calls=%async_computation.17 | async-start | bytes 4325376 | tf_op jit(solution)/shard_map/reduce_scatter | solution.py:358
  714.0 845.3 %reduce-scatter.10.cloned.1.call-start = ((), (), s32[]{:S(2)}) async-start(), calls=%async_computation.9 | async-start | bytes 7299072 | tf_op jit(solution)/shard_map/reduce_scatter | solution.py:346
  714.7 986.9 %reduce-scatter.14.cloned.1.call-start = ((), (), s32[]{:S(2)}) async-start(), calls=%async_computation.11 | async-start | bytes 9732096 | tf_op jit(solution)/shard_map/reduce_scatter | solution.py:349
  715.5 1127.3 %reduce-scatter.16.cloned.1.call-start = ((), (), s32[]{:S(2)}) async-start(), calls=%async_computation.12 | async-start | bytes 9732096 | tf_op jit(solution)/shard_map/reduce_scatter | solution.py:350
  (588 other events, 2972.3 us)
Sparse Core Ops, SparseCore 0:
  710.9 99.6 reduce-scatter.17
  813.4 134.2 reduce-scatter.21
  954.4 94.9 reduce-scatter.11
  1055.2 100.5 reduce-scatter.19
  1158.5 139.5 reduce-scatter.23
  1300.8 136.9 reduce-scatter.25
  1444.1 115.1 reduce-scatter.9
  1566.8 134.8 reduce-scatter.13
  1708.1 134.5 reduce-scatter.15
where the time goes:
time: 1850 us
  waiting for transfers between devices  1090 us (59%)
  matrix products  541 us (29%)
  local copies, waits for them, and re-layouts  82.8 us (4%)
  other arithmetic  70.3 us (4%)
  blocking collectives  42.2 us (2%)
    dot_general x54, matrix products, outer_sum(): lax.dot_general(flat_left, flat_right, (((0,), (0,)), ((), ())), preferre...  209 us
    reduce_scatter x1, waiting for transfers between devices, local(): lax.psum_scatter(totals[4], ('dp', 'seq'), scatter_dimension=0, tiled=True)  142 us
    reduce_scatter x1, waiting for transfers between devices, local(): lax.psum_scatter(totals[12], ('dp', 'seq'), scatter_dimension=0, tiled=True)  142 us
    reduce_scatter x1, waiting for transfers between devices, local(): lax.psum_scatter(totals[5], ('dp', 'seq'), scatter_dimension=0, tiled=True)  141 us
    reduce_scatter x1, waiting for transfers between devices, local(): lax.psum_scatter(totals[13], ('dp', 'seq'), scatter_dimension=0, tiled=True)  140 us
    reduce_scatter x1, waiting for transfers between devices, local(): lax.psum_scatter(totals[10], ('dp', 'seq'), scatter_dimension=0, tiled=True)  137 us
    dot_general x54, matrix products, contract(): jnp.einsum('...i,ij->...j', operand, matrix, preferred_element_type=jnp.f...  123 us
    reduce_scatter x1, waiting for transfers between devices, local(): lax.psum_scatter(totals[1], ('dp', 'seq'), scatter_dimension=0, tiled=True)  121 us
  transfers between devices with their start and end apart: 9, of which 9 were waited for; matrix products, arithmetic and copies ran while one was open for 0% of the time, Pallas kernels for 0%

commit v1 on v0

--- a/solution.py
+++ b/solution.py
@@ -1,8 +1,11 @@
+import functools
 import math
 
 import jax
 import jax.numpy as jnp
 from jax import lax
+from jax.experimental import pallas as pl
+from jax.experimental.pallas import tpu as pltpu
 from jax.sharding import PartitionSpec as P
 
 HEADS = 12
@@ -244,8 +247,11 @@
     places = jnp.arange(PATCHES)
     matches = (positions[:, :, None] == places[None, None, :]) & live_slots[:, :, None]
     covered = jnp.any(matches, axis=1)
-    slot_index = jnp.sum(jnp.where(matches, jnp.arange(slot_total)[None, :, None], 0), axis=1)
-    picked = jnp.take_along_axis(embedded, slot_index[:, :, None], axis=1)
+    pick = matches.astype(jnp.bfloat16)
+    high = embedded.astype(jnp.bfloat16)
+    low = (embedded - high.astype(jnp.float32)).astype(jnp.bfloat16)
+    picked = jnp.einsum("bjp,bjw->bpw", pick, high, preferred_element_type=jnp.float32)
+    picked = picked + jnp.einsum("bjp,bjw->bpw", pick, low, preferred_element_type=jnp.float32)
     filled = jnp.where(covered[:, :, None], picked, mask_token.astype(jnp.float32))
     filled = filled + position_table(PATCHES, embedded.shape[-1])
     filled_low = filled.astype(jnp.bfloat16)
@@ -257,14 +263,169 @@
     mask_term = jnp.sum(
         jnp.where(covered[:, :, None], 0.0, grad_filled).reshape(-1, grad_filled.shape[-1]), axis=0
     )
-    grad_embedded = jnp.take_along_axis(grad_filled, positions[:, :, None], axis=1)
-    grad_embedded = jnp.where(live_slots[:, :, None], grad_embedded, 0.0).astype(jnp.bfloat16)
+    grad_embedded = jnp.einsum(
+        "bjp,bpw->bjw", pick, grad_filled.astype(jnp.bfloat16), preferred_element_type=jnp.float32
+    ).astype(jnp.bfloat16)
     embed_term = outer_sum(encoded_low, grad_embedded)
     grad_encoded = contract_back(grad_embedded, embed_weight)
     enc_back = block_backward(grad_encoded, enc_kept, enc_weights, HEADS)
     grad_input = enc_back[0]
     enc_terms = enc_back[1:] + (embed_term, mask_term)
     return (dec_piece, grad_input, tuple(enc_terms) + tuple(dec_terms))
+
+
+MESH = pl.DeviceIdType.MESH
+W = 256
+STEP = 64
+FLOWS = ((0, 24, "xyls"), (24, 24, "yxls"), (48, 8, "lsxy"), (56, 8, "lsyx"))
+DIMS = "slyx"
+
+def coords():
+    seq = lax.axis_index("seq"); dp = lax.axis_index("dp")
+    return {"s": dp // 4, "l": (dp // 2) % 2, "y": dp % 2, "x": seq // 2, "c": seq % 2}
+
+def partner(here, dim):
+    other = dict(here); other[dim] = 1 - here[dim]
+    return (other["s"] * 4 + other["l"] * 2 + other["y"], other["x"] * 2 + other["c"])
+
+def comm_scratch(nt):
+    sc = [pltpu.VMEM((nt, 2, 2, 2, 2, STEP, W), jnp.float32)]
+    for _, rows, order in FLOWS:
+        for k in range(1, 5):
+            sc.append(pltpu.VMEM((nt,) + (2,) * (4 - k) + (rows, W), jnp.float32))
+    sc.append(pltpu.VMEM((2, 2, 2, 2, 2, STEP, W), jnp.float32))
+    sc += [pltpu.SemaphoreType.DMA((nt, 17)), pltpu.SemaphoreType.DMA((nt, 17)), pltpu.SemaphoreType.DMA((2,))]
+    return sc
+
+class Comm:
+    def __init__(self, g_ref, out_ref, scratch, nt):
+        self.g, self.out, self.nt = g_ref, out_ref, nt
+        self.land0 = scratch[0]
+        self.lands = [scratch[1 + 4 * f: 5 + 4 * f] for f in range(4)]
+        self.own, self.ssem, self.rsem, self.lsem = scratch[17:21]
+        self.here = coords()
+
+    def barrier(self):
+        bar = pltpu.get_barrier_semaphore()
+        for d in "c" + DIMS:
+            pl.semaphore_signal(bar, inc=1, device_id=partner(self.here, d), device_id_type=MESH)
+        pl.semaphore_wait(bar, 5)
+
+    def core_copy(self, t):
+        rows = pl.ds(pl.multiple_of(t * STEP, STEP), STEP)
+        return pltpu.make_async_remote_copy(
+            src_ref=self.g.at[:, :, :, :, 1 - self.here["c"], rows], dst_ref=self.land0.at[t],
+            send_sem=self.ssem.at[t, 16], recv_sem=self.rsem.at[t, 16],
+            device_id=partner(self.here, "c"), device_id_type=MESH)
+
+    def own_copy(self, t):
+        rows = pl.ds(pl.multiple_of(t * STEP, STEP), STEP)
+        return pltpu.make_async_copy(self.g.at[:, :, :, :, self.here["c"], rows], self.own.at[t % 2], self.lsem.at[t % 2])
+
+    def source(self, t, f, k, mine):
+        off, rows, order = FLOWS[f]
+        left = "".join(d for d in DIMS if d not in order[:k])
+        d = order[k]
+        pick = tuple((self.here[d] if mine else 1 - self.here[d]) if e == d else slice(None) for e in left)
+        if k == 0:
+            return self.land0.at[(t,) + pick + (pl.ds(off, rows),)]
+        return self.lands[f][k - 1].at[(t,) + pick]
+
+    def copy(self, t, f, k):
+        d = FLOWS[f][2][k]
+        i = f * 4 + k
+        return pltpu.make_async_remote_copy(
+            src_ref=self.source(t, f, k, False), dst_ref=self.lands[f][k].at[t],
+            send_sem=self.ssem.at[t, i], recv_sem=self.rsem.at[t, i],
+            device_id=partner(self.here, d), device_id_type=MESH)
+
+    def stage(self, k, t):
+        if k == 0:
+            self.core_copy(t).start()
+            self.own_copy(t).start()
+        elif k == 1:
+            self.own_copy(t).wait()
+            self.core_copy(t).wait()
+            self.land0[t] += self.own[t % 2]
+            for f in range(4):
+                self.copy(t, f, 0).start()
+        else:
+            for f in range(4):
+                self.copy(t, f, k - 2).wait()
+                land = self.lands[f][k - 2]
+                kept = self.source(t, f, k - 2, True)
+                if k < 5:
+                    land[t] += kept[...]
+                    self.copy(t, f, k - 1).start()
+                else:
+                    off, rows, _ = FLOWS[f]
+                    at = pl.ds(pl.multiple_of(t * STEP + off, 8), rows)
+                    self.out[at] = land[t] + kept[...]
+
+    def step(self, t):
+        for k in range(6):
+            p = t - k
+            @pl.when((p >= 0) & (p < self.nt))
+            def _():
+                self.stage(k, p)
+
+def comm_only_kernel(nt, g_ref, out_ref, *scratch):
+    comm = Comm(g_ref, out_ref, scratch, nt)
+    comm.barrier()
+    def body(t, _):
+        comm.step(t); return 0
+    lax.fori_loop(0, nt + 5, body, 0)
+
+def reduce_scatter(g, nt, cid):
+    return pl.pallas_call(functools.partial(comm_only_kernel, nt),
+        out_shape=jax.ShapeDtypeStruct((nt * STEP, W), jnp.float32),
+        in_specs=[pl.BlockSpec(memory_space=pl.ANY)], out_specs=pl.BlockSpec(memory_space=pltpu.VMEM),
+        scratch_shapes=comm_scratch(nt), name="comm",
+        compiler_params=pltpu.CompilerParams(collective_id=cid, has_side_effects=True, vmem_limit_bytes=60 * 2**20))(g)
+
+
+GROUPS = (((13, 12, 10, 9), (8, 11)), ((6, 5, 4, 2, 1), (0, 3, 7)))
+
+
+def reduce_group(totals, matrices, vectors, call):
+    parts = lax.axis_size("dp") * lax.axis_size("seq")
+    blocks = []
+    for i in matrices:
+        rows, columns = totals[i].shape
+        block = totals[i].reshape(parts, rows // parts, columns // W, W)
+        blocks.append(block.transpose(0, 2, 1, 3).reshape(parts, -1, W))
+    vector = jnp.concatenate([totals[i].reshape(parts, -1) for i in vectors], axis=1)
+    blocks.append(jnp.pad(vector, ((0, 0), (0, 8 * W - vector.shape[1]))).reshape(parts, 8, W))
+    used = sum(block.shape[1] for block in blocks)
+    steps = -(-used // STEP)
+    blocks.append(jnp.zeros((parts, steps * STEP - used, W), jnp.float32))
+    whole = jnp.concatenate(blocks, axis=1).reshape(2, 2, 2, 2, 2, steps * STEP, W)
+    mine = reduce_scatter(whole, steps, call)
+    out = {}
+    at = 0
+    for i in matrices:
+        rows, columns = totals[i].shape[0] // parts, totals[i].shape[1]
+        size = rows * columns // W
+        out[i] = mine[at : at + size].reshape(columns // W, rows, W).transpose(1, 0, 2).reshape(rows, columns)
+        at += size
+    vector = mine[at]
+    at = 0
+    for i in vectors:
+        size = totals[i].shape[0] // parts
+        out[i] = vector[at : at + size]
+        at += size
+    return out
+
+
+def reduce_all(totals):
+    if (lax.axis_size("dp"), lax.axis_size("seq")) != (8, 4):
+        return tuple(
+            lax.psum_scatter(total, ("dp", "seq"), scatter_dimension=0, tiled=True) for total in totals
+        )
+    out = {}
+    for call, (matrices, vectors) in enumerate(GROUPS):
+        out.update(reduce_group(totals, matrices, vectors, call))
+    return tuple(out[i] for i in range(len(totals)))
 
 
 def local(
@@ -319,44 +480,10 @@
         dec_up_weight,
         dec_down_weight,
     )
-    totals = tuple((jnp.zeros(param.shape, jnp.float32) for param in all_params))
-
-    def one_micro(running, pieces):
-        enc_rows, counts, positions, cot_rows = pieces
-        dec_piece, grad_input, terms = micro_step(
-            enc_rows,
-            counts,
-            positions,
-            cot_rows,
-            enc_weights,
-            embed_weight,
-            mask_token,
-            dec_weights,
-        )
-        running = tuple((total + term for total, term in zip(running, terms)))
-        return (running, (dec_piece, grad_input))
-
-    totals, (dec_pieces, input_grads) = lax.scan(
-        one_micro,
-        totals,
-        (enc_input[:, None], keep_count[:, None], keep_positions[:, None], cotangent[:, None]),
-    )
-    totals = (
-        lax.psum_scatter(totals[0], ("dp", "seq"), scatter_dimension=0, tiled=True),
-        lax.psum_scatter(totals[1], ("dp", "seq"), scatter_dimension=0, tiled=True),
-        lax.psum_scatter(totals[2], ("dp", "seq"), scatter_dimension=0, tiled=True),
-        lax.psum_scatter(totals[3], ("dp", "seq"), scatter_dimension=0, tiled=True),
-        lax.psum_scatter(totals[4], ("dp", "seq"), scatter_dimension=0, tiled=True),
-        lax.psum_scatter(totals[5], ("dp", "seq"), scatter_dimension=0, tiled=True),
-        lax.psum_scatter(totals[6], ("dp", "seq"), scatter_dimension=0, tiled=True),
-        lax.psum_scatter(totals[7], ("dp", "seq"), scatter_dimension=0, tiled=True),
-        lax.psum_scatter(totals[8], ("dp", "seq"), scatter_dimension=0, tiled=True),
-        lax.psum_scatter(totals[9], ("dp", "seq"), scatter_dimension=0, tiled=True),
-        lax.psum_scatter(totals[10], ("dp", "seq"), scatter_dimension=0, tiled=True),
-        lax.psum_scatter(totals[11], ("dp", "seq"), scatter_dimension=0, tiled=True),
-        lax.psum_scatter(totals[12], ("dp", "seq"), scatter_dimension=0, tiled=True),
-        lax.psum_scatter(totals[13], ("dp", "seq"), scatter_dimension=0, tiled=True),
-    )
+    dec_pieces, input_grads, totals = micro_step(
+        enc_input, keep_count, keep_positions, cotangent, enc_weights, embed_weight, mask_token, dec_weights
+    )
+    totals = reduce_all(totals)
     dec_output = dec_pieces.reshape(cotangent.shape)
     enc_input_grad = input_grads.reshape(enc_input.shape)
     return (

time: 1850 us -> 716 us (0.39)
  waiting for transfers between devices: 1090 us -> 0 us
  matrix products: 541 us -> 197 us
  Pallas kernels: 0 us -> 195 us
  local copies, waits for them, and re-layouts: 82.8 us -> 235 us
  blocking collectives: 42.2 us -> 0 us
    reduce_scatter x9 -> x0, waiting for transfers between devices: 1080 us -> none  [the longest x1 142 us: local(): lax.psum_scatter(totals[4], ('dp', 'seq'), scatter_dimension=0, tiled=True)]
    pallas_call x0 -> x2, Pallas kernels: none -> 195 us  [reduce_scatter(): pl.pallas_call(functools.partial(comm_only_kernel, nt), out_shape=jax.Sha...]
    dot_general x54 -> x9, matrix products: 209 us -> 35.8 us  [outer_sum(): lax.dot_general(flat_left, flat_right, (((0,), (0,)), ((), ())), preferre...]
    dot_general x54 -> x9, matrix products: 123 us -> 24.5 us  [contract(): jnp.einsum('...i,ij->...j', operand, matrix, preferred_element_type=jnp.f...]
    reshape x0 -> x34, local copies, waits for them, and re-layouts: none -> 75.6 us  [the longest x10 31.5 us: outer_sum(): flat_right = gradient.reshape(-1, gradient.shape[-1])]
    dot_general x54 -> x9, matrix products: 114 us -> 48.9 us  [contract_back(): jnp.einsum('...j,ij->...i', gradient, matrix, preferred_element_type=jnp....]
    while x1212 -> x0, local copies, waits for them, and re-layouts: 49.8 us -> none
    convert_element_type x12 -> x8, other arithmetic: 0.94 us -> 46 us  [the longest x2 41.5 us: mlp_forward(): active_low = exact_gelu(pre_act).astype(jnp.bfloat16)]
  transfers between devices with their start and end apart: 9 -> 0, of which waited for: 9 -> 0; matrix products, arithmetic and copies ran while one was open for 0% -> 0% of each run, Pallas kernels for 0% -> 0%
where the time goes in v1:
time: 716 us; the launch traced here: 710 us
  local copies, waits for them, and re-layouts  235 us (33%)
  matrix products  197 us (28%)
  Pallas kernels  195 us (27%)
  other arithmetic  80.4 us (11%)
    pallas_call x2, Pallas kernels, reduce_scatter(): pl.pallas_call(functools.partial(comm_only_kernel, nt), out_shape=jax.Sha...  195 us
    dot_general x9, matrix products, contract_back(): jnp.einsum('...j,ij->...i', gradient, matrix, preferred_element_type=jnp....  48.9 us
    convert_element_type x2, other arithmetic, mlp_forward(): active_low = exact_gelu(pre_act).astype(jnp.bfloat16)  41.5 us
    unnamed x208, local copies, waits for them, and re-layouts  38.6 us
    dot_general x9, matrix products, outer_sum(): lax.dot_general(flat_left, flat_right, (((0,), (0,)), ((), ())), preferre...  35.8 us
    reshape x10, local copies, waits for them, and re-layouts, outer_sum(): flat_right = gradient.reshape(-1, gradient.shape[-1])  31.5 us
    dot_general x8, local copies, waits for them, and re-layouts, outer_sum(): lax.dot_general(flat_left, flat_right, (((0,), (0,)), ((), ())), preferre...  27.9 us
    dot_general x9, matrix products, contract(): jnp.einsum('...i,ij->...j', operand, matrix, preferred_element_type=jnp.f...  24.5 us

profile of v1, /device:TPU:0, one launch (start us, length us, event | category | flops | bytes accessed | tf_op | source)
XLA Modules:
  0.0 710.2 jit_solution(10859035301134100812)
XLA Ops:
  19.6 6.1 fusion.154
  32.4 5.1 fusion.90
  37.5 18.3 %multiply_convert_fusion.2 = (bf16[6,98,3072]{2,1,0:T(8,128)(2,1)S(1)}, f32[6,98,3072]{2,1,0:T(8,128)}) fusion(f32[6,98,3072]{2,1,0:T(8,128)S(1)} %get-tuple-element.64, u8[98,3072]{1,0:T(8,128)(4,1)S(1)} %get-tuple-element.19, u8[98,3072]{1,0:T(8,128)(4,1)S(1)} %get-tuple-element.18), kind=kLoop, calls=%fused_computation.38 | loop fusion | flops 126443520 | bytes 18665472 | tf_op jit(solution)/shard_map/convert_element_type | solution.py:154
  76.4 13.2 %fusion.156 = (f32[6,16,196]{2,1,0:T(8,128)}, f32[6,16,196,196]{2,3,1,0:T(8,128)}) fusion(bf16[6,196,16,32]{1,3,2,0:T(8,128)(2,1)} %bitcast.391, bf16[6,196,16,32]{1,3,2,0:T(8,128)(2,1)} %bitcast.393), kind=kOutput, calls=%fused_computation.271 | convolution fusion | flops 247091904 | bytes 17235456 | tf_op jit(solution)/shard_map/sub | solution.py:98
  89.7 9.2 %fusion.92 = bf16[6,16,32,196]{3,2,1,0:T(8,128)(2,1)S(1)} fusion(bf16[6,196,16,32]{1,3,2,0:T(8,128)(2,1)} %bitcast.422, f32[6,16,196,196]{2,3,1,0:T(8,128)} %get-tuple-element.68, f32[6,16,196]{2,1,0:T(8,128)} %get-tuple-element.67), kind=kOutput, calls=%fused_computation.160 | convolution fusion | flops 244005888 | bytes 17235456 | tf_op jit(solution)/shard_map/bhqk,bkhd->bqhd/dot_general | solution.py:101
  102.4 5.1 fusion.66
  107.5 23.2 %multiply_convert_fusion.1 = (bf16[6,196,2048]{2,1,0:T(8,128)(2,1)S(1)}, f32[6,196,2048]{2,1,0:T(8,128)}) fusion(f32[6,196,2048]{2,1,0:T(8,128)S(1)} %get-tuple-element.71, u8[196,2048]{1,0:T(8,128)(4,1)S(1)} %get-tuple-element.17, u8[196,2048]{1,0:T(8,128)(4,1)S(1)} %get-tuple-element.16), kind=kLoop, calls=%fused_computation.16 | loop fusion | flops 168591360 | bytes 24887296 | tf_op jit(solution)/shard_map/convert_element_type | solution.py:154
  134.7 9.8 %add_convert_fusion = bf16[6,196,2048]{2,1,0:T(8,128)(2,1)} fusion(f32[6,196,2048]{2,1,0:T(8,128)} %get-tuple-element.37, f32[6,196,2048]{2,1,0:T(8,128)S(1)} %get-tuple-element.71, bf16[6,196,512]{2,1,0:T(8,128)(2,1)S(1)} %copy-done.15, bf16[2048,512]{1,0:T(8,128)(2,1)S(1)} %copy-done.85), kind=kOutput, calls=%fused_computation.15 | convolution fusion | flops 2499969024 | bytes 27385856 | tf_op jit(solution)/shard_map/...j,ij->...i/dot_general | solution.py:42
  144.6 6.5 multiply_reduce_fusion.3
  158.0 11.3 %fusion.95 = bf16[6,16,32,196]{3,2,1,0:T(8,128)(2,1)} fusion(bf16[6,196,16,32]{1,3,2,0:T(8,128)(2,1)} %bitcast.424, f32[6,16,196,196]{2,3,1,0:T(8,128)} %get-tuple-element.68, f32[6,16,196]{2,1,0:T(8,128)} %get-tuple-element.67), kind=kOutput, calls=%fused_computation.161 | convolution fusion | flops 244005888 | bytes 17235456 | tf_op jit(solution)/shard_map/bhqk,bqhd->bkhd/dot_general | solution.py:121
  171.9 16.8 %multiply_reduce_fusion = (f32[6,16,196]{2,1,0:T(8,128)S(1)}, f32[6,16,196,196]{2,3,1,0:T(8,128)}) fusion(f32[6,16,196,196]{2,3,1,0:T(8,128)} %get-tuple-element.68, f32[6,16,196]{2,1,0:T(8,128)} %get-tuple-element.67, bf16[6,196,16,32]{1,3,2,0:T(8,128)(2,1)} %bitcast.425, bf16[6,196,16,32]{1,3,2,0:T(8,128)(2,1)} %bitcast.423), kind=kOutput, calls=%fused_computation.3 | convolution fusion | flops 247072896 | bytes 32062464 | tf_op jit(solution)/shard_map/bqhd,bkhd->bhqk/dot_general | solution.py:124
  188.7 14.1 %multiply_convert_fusion = bf16[6,16,196,196]{2,3,1,0:T(8,128)(2,1)S(1)} fusion(f32[6,16,196,196]{2,3,1,0:T(8,128)} %get-tuple-element.74, f32[6,16,196]{2,1,0:T(8,128)S(1)} %get-tuple-element.73, f32[6,16,196,196]{2,3,1,0:T(8,128)} %get-tuple-element.68, f32[6,16,196]{2,1,0:T(8,128)S(1)} %copy-done.51), kind=kLoop, calls=%fused_computation.2 | loop fusion | flops 14751744 | bytes 37029888 | tf_op jit(solution)/shard_map/convert_element_type | solution.py:130
  209.5 7.3 %multiply_convert_fusion.5 = bf16[6,16,32,196]{3,2,1,0:T(8,128)(2,1)} fusion(bf16[6,196,16,32]{1,3,2,0:T(8,128)(2,1)} %bitcast.394, bf16[6,16,196,196]{2,3,1,0:T(8,128)(2,1)} %copy-done.1), kind=kOutput, calls=%fused_computation.87 | convolution fusion | flops 237232128 | bytes 9784320 | tf_op jit(solution)/shard_map/bhqk,bkhd->bqhd/dot_general | solution.py:132
  219.5 5.7 fusion.63
  229.6 8.8 %add_convert_fusion.1 = bf16[6,98,3072]{2,1,0:T(8,128)(2,1)S(1)} fusion(f32[6,98,3072]{2,1,0:T(8,128)} %get-tuple-element.39, f32[6,98,3072]{2,1,0:T(8,128)S(1)} %bitcast.385, bf16[6,98,768]{2,1,0:T(8,128)(2,1)S(1)} %get-tuple-element.76, bf16[3072,768]{1,0:T(8,128)(2,1)} %param.26), kind=kOutput, calls=%fused_computation.37 | convolution fusion | flops 2799820800 | bytes 23685120 | tf_op jit(solution)/shard_map/...j,ij->...i/dot_general | solution.py:42
  238.5 8.0 %multiply_reduce_fusion.8 = (f32[768]{0:T(1024)}, f32[6,98]{1,0:T(8,128)S(1)}, f32[6,98]{1,0:T(8,128)S(1)}, f32[6,98,768]{2,1,0:T(8,128)S(1)}) fusion(f32[6,98,768]{2,1,0:T(8,128)S(1)} %copy-done.8, f32[6,98]{1,0:T(8,128)S(1)} %copy-done.68, f32[6,98]{1,0:T(8,128)S(1)} %copy-done.59, f32[768]{0:T(1024)S(1)} %copy-done.66, ...), kind=kOutput, calls=%fused_computation.147 | convolution fusion | flops 2778142976 | bytes 11959488 | tf_op jit(solution)/shard_map/...j,ij->...i/dot_general | solution.py:42
  253.7 4.9 convolution_convert_fusion.3
  278.8 5.6 fusion.85
  303.0 5.9 copy.108
  313.3 6.4 fusion.159
  319.7 4.7 constant_dynamic-update-slice_fusion.4
  333.1 5.9 copy.112
  339.0 6.3 fusion.160
  345.3 4.9 constant_dynamic-update-slice_fusion.3
  403.9 130.1 %comm.2 = f32[960,256]{1,0:T(8,128)} custom-call(f32[2,2,2,2,2,960,256]{6,5,4,3,2,1,0:T(8,128)} %broadcast_dynamic-update-slice_fusion.1.g_ref), custom_call_target="tpu_custom_call" | custom-call | tf_op jit(solution)/shard_map/comm/pallas_call | solution.py:380
  542.7 5.9 reshape.494
  548.5 7.7 %copy.127 = bf16[2048,1176]{1,0:T(8,128)(2,1)} copy(bf16[2048,1176]{0,1:T(8,128)(2,1)} %bitcast.372) | data formatting | bytes 9633792 | tf_op jit(solution)/shard_map/dot_general | solution.py:48
  558.6 5.1 fusion.106
  570.8 5.9 reshape.497
  576.6 5.5 fusion.24
  586.9 4.2 convert_element_type.228
  638.2 65.2 %comm.3 = f32[448,256]{1,0:T(8,128)} custom-call(f32[2,2,2,2,2,448,256]{6,5,4,3,2,1,0:T(8,128)} %broadcast_dynamic-update-slice_fusion.g_ref), custom_call_target="tpu_custom_call" | custom-call | tf_op jit(solution)/shard_map/comm/pallas_call | solution.py:380
  (352 shorter events, 265.2 us)
Async XLA Ops:
  0.6 7.1 copy-start
  0.7 6.7 copy-start.9
  14.8 45.9 %copy-start.79 = (pred[6,98]{1,0:T(8,128)(4,1)}, pred[6,98]{1,0:T(8,128)(4,1)S(1)}, u32[]{:S(2)}) copy-start(pred[6,98]{1,0:T(8,128)(4,1)S(1)} %iota_compare_fusion.3) | copy-start | bytes 1768
  30.0 25.8 %copy-start.7 = (f32[6,98,768]{2,1,0:T(8,128)}, f32[6,98,768]{2,1,0:T(8,128)S(1)}, u32[]{:S(2)}) copy-start(f32[6,98,768]{2,1,0:T(8,128)S(1)} %get-tuple-element.63) | copy-start | bytes 5419012
  31.5 24.4 %slice-start.3 = ((s8[4718592]{0:T(1024)(128)(4,1)}), s8[4194304]{0:T(1024)(128)(4,1)S(1)}, s32[]{:S(2)}) async-start(s8[4718592]{0:T(1024)(128)(4,1)} %bitcast.464), calls=%async_computation.3 | async-start | bytes 8388608
  32.4 23.5 %slice-start.4 = ((s8[4718592]{0:T(1024)(128)(4,1)}), s8[524288]{0:T(1024)(128)(4,1)S(1)}, s32[]{:S(2)}) async-start(s8[4718592]{0:T(1024)(128)(4,1)} %bitcast.464), calls=%async_computation.4 | async-start | bytes 1048576
  37.5 18.3 %copy-start.20 = (f32[6,98,3072]{2,1,0:T(8,128)}, f32[6,98,3072]{2,1,0:T(8,128)S(1)}, u32[]{:S(2)}) copy-start(f32[6,98,3072]{2,1,0:T(8,128)S(1)} %get-tuple-element.64) | copy-start | bytes 21676036
  89.7 9.3 %copy-start.5 = (bf16[6,196,512]{2,1,0:T(8,128)(2,1)S(1)}, bf16[6,196,512]{2,1,0:T(8,128)(2,1)}, u32[]{:S(2)}) copy-start(bf16[6,196,512]{2,1,0:T(8,128)(2,1)} %copy-done.4) | copy-start | bytes 3612676
  89.7 9.3 %copy-start.46 = (bf16[512,512]{1,0:T(8,128)(2,1)S(1)}, bf16[512,512]{1,0:T(8,128)(2,1)}, u32[]{:S(2)}) copy-start(bf16[512,512]{1,0:T(8,128)(2,1)} %param.31) | copy-start | bytes 1572868
  99.9 51.1 %copy-start.2 = (f32[6,196,512]{2,1,0:T(8,128)}, f32[6,196,512]{2,1,0:T(8,128)S(1)}, u32[]{:S(2)}) copy-start(f32[6,196,512]{2,1,0:T(8,128)S(1)} %get-tuple-element.70) | copy-start | bytes 7225348
  100.0 51.1 %copy-start.73 = (f32[512]{0:T(512)}, f32[512]{0:T(512)S(1)}, u32[]{:S(2)}) copy-start(f32[512]{0:T(512)S(1)} %convert_element_type.210) | copy-start | bytes 6148
  100.6 50.5 %copy-start.49 = (f32[6,196]{1,0:T(8,128)}, f32[6,196]{1,0:T(8,128)S(1)}, u32[]{:S(2)}) copy-start(f32[6,196]{1,0:T(8,128)S(1)} %add_rsqrt_fusion) | copy-start | bytes 14116
  107.5 23.3 %copy-start.85 = (bf16[2048,512]{1,0:T(8,128)(2,1)S(1)}, bf16[2048,512]{1,0:T(8,128)(2,1)}, u32[]{:S(2)}) copy-start(bf16[2048,512]{1,0:T(8,128)(2,1)} %param.34) | copy-start | bytes 6291460
  171.9 16.8 %copy-start.51 = (f32[6,16,196]{2,1,0:T(8,128)S(1)}, f32[6,16,196]{2,1,0:T(8,128)}, u32[]{:S(2)}) copy-start(f32[6,16,196]{2,1,0:T(8,128)} %get-tuple-element.67) | copy-start | bytes 225796
  188.7 14.1 %copy-start.23 = (bf16[6,196,512]{1,2,0:T(8,128)(2,1)S(1)}, bf16[6,196,512]{1,2,0:T(8,128)(2,1)}, u32[]{:S(2)}) copy-start(bf16[6,196,512]{1,2,0:T(8,128)(2,1)} %copy.88) | copy-start | bytes 3612676
  209.5 9.9 %copy-start.48 = (f32[6,196]{1,0:T(8,128)S(1)}, f32[6,196]{1,0:T(8,128)}, u32[]{:S(2)}) copy-start(f32[6,196]{1,0:T(8,128)} %copy-done.47) | copy-start | bytes 14116
  219.4 5.8 copy-start.6
  219.4 5.9 copy-start.16
  219.4 5.8 copy-start.18
  219.4 5.8 copy-start.50
  219.5 5.8 copy-start.53
  229.5 9.0 %copy-start.36 = (bf16[6,98,768]{2,1,0:T(8,128)(2,1)}, bf16[6,98,768]{2,1,0:T(8,128)(2,1)S(1)}, u32[]{:S(2)}) copy-start(bf16[6,98,768]{2,1,0:T(8,128)(2,1)S(1)} %get-tuple-element.76) | copy-start | bytes 2709508
  229.6 8.9 %copy-start.8 = (f32[6,98,768]{2,1,0:T(8,128)S(1)}, f32[6,98,768]{2,1,0:T(8,128)}, u32[]{:S(2)}) copy-start(f32[6,98,768]{2,1,0:T(8,128)} %copy-done.7) | copy-start | bytes 5419012
  229.6 8.9 %copy-start.59 = (f32[6,98]{1,0:T(8,128)S(1)}, f32[6,98]{1,0:T(8,128)}, u32[]{:S(2)}) copy-start(f32[6,98]{1,0:T(8,128)} %copy-done.58) | copy-start | bytes 7060
  229.6 8.9 %copy-start.66 = (f32[768]{0:T(1024)S(1)}, f32[768]{0:T(1024)}, u32[]{:S(2)}) copy-start(f32[768]{0:T(1024)} %copy-done.65) | copy-start | bytes 9220
  229.6 8.9 %copy-start.68 = (f32[6,98]{1,0:T(8,128)S(1)}, f32[6,98]{1,0:T(8,128)}, u32[]{:S(2)}) copy-start(f32[6,98]{1,0:T(8,128)} %copy-done.67) | copy-start | bytes 7060
  238.5 8.0 %copy-start.32 = (bf16[6,98,3072]{2,1,0:T(8,128)(2,1)}, bf16[6,98,3072]{2,1,0:T(8,128)(2,1)S(1)}, u32[]{:S(2)}) copy-start(bf16[6,98,3072]{2,1,0:T(8,128)(2,1)S(1)} %add_convert_fusion.1) | copy-start | bytes 10838020
  272.3 6.4 copy-start.63
  272.3 6.5 copy-start.70
  272.3 6.5 copy-start.72
  534.0 7.5 %slice-start.2 = ((f32[960,256]{1,0:T(8,128)}), f32[48,256]{1,0:T(8,128)S(1)}, s32[]{:S(2)}) async-start(f32[960,256]{1,0:T(8,128)} %comm.2), calls=%async_computation.2 | async-start | bytes 98304 | tf_op jit(solution)/shard_map/slice | solution.py:409
  534.0 8.1 %copy-start.37 = (f32[960,256]{1,0:T(8,128)S(1)}, f32[960,256]{1,0:T(8,128)}, u32[]{:S(2)}) copy-start(f32[960,256]{1,0:T(8,128)} %comm.2) | copy-start | bytes 2949124
  (64 other events, 187.1 us)

commit v2 on v0

--- a/solution.py
+++ b/solution.py
@@ -1,8 +1,12 @@
+import functools
 import math
 
 import jax
 import jax.numpy as jnp
+import numpy as np
 from jax import lax
+from jax.experimental import pallas as pl
+from jax.experimental.pallas import tpu as pltpu
 from jax.sharding import PartitionSpec as P
 
 HEADS = 12
@@ -319,27 +323,8 @@
         dec_up_weight,
         dec_down_weight,
     )
-    totals = tuple((jnp.zeros(param.shape, jnp.float32) for param in all_params))
-
-    def one_micro(running, pieces):
-        enc_rows, counts, positions, cot_rows = pieces
-        dec_piece, grad_input, terms = micro_step(
-            enc_rows,
-            counts,
-            positions,
-            cot_rows,
-            enc_weights,
-            embed_weight,
-            mask_token,
-            dec_weights,
-        )
-        running = tuple((total + term for total, term in zip(running, terms)))
-        return (running, (dec_piece, grad_input))
-
-    totals, (dec_pieces, input_grads) = lax.scan(
-        one_micro,
-        totals,
-        (enc_input[:, None], keep_count[:, None], keep_positions[:, None], cotangent[:, None]),
+    dec_pieces, input_grads, totals = micro_step(
+        enc_input, keep_count, keep_positions, cotangent, enc_weights, embed_weight, mask_token, dec_weights
     )
     totals = (
         lax.psum_scatter(totals[0], ("dp", "seq"), scatter_dimension=0, tiled=True),
@@ -379,6 +364,765 @@
     )
 
 
+MESH = pl.DeviceIdType.MESH
+BF = jnp.bfloat16
+F32 = jnp.float32
+LANES = 128
+TILE = 256
+CHUNK = 48
+VMEM_BYTES = 62 * 2**20
+STEP = 72
+FLOWS = ((0, 32, "xyls"), (32, 24, "yxls"), (56, 8, "lsxy"), (64, 8, "lsyx"))
+DIMS = "slyx"
+
+
+def padded(count, multiple):
+    return -(-count // multiple) * multiple
+
+
+def nn(left, right):
+    return lax.dot_general(left, right, (((1,), (0,)), ((), ())), preferred_element_type=F32)
+
+
+def nt(left, right):
+    return lax.dot_general(left, right, (((1,), (1,)), ((), ())), preferred_element_type=F32)
+
+
+def tn(left, right):
+    return lax.dot_general(left, right, (((0,), (0,)), ((), ())), preferred_element_type=F32)
+
+
+def columns(tile):
+    return pl.ds(pl.multiple_of(tile * TILE, TILE), TILE)
+
+
+def each(count, body):
+    lax.fori_loop(0, count, lambda index, carry: (body(index), carry)[1], 0)
+
+
+def gelu_pair(values):
+    reach = jnp.abs(values)
+    point = 1.0 / (1.0 + 0.23164189 * reach)
+    decay = jnp.exp(-0.5 * values * values)
+    tail = 0.5307027145 * point - 0.7265760135
+    tail = tail * point + 0.710706870
+    tail = tail * point - 0.142248368
+    tail = tail * point + 0.127414796
+    tail = tail * point * decay
+    below = jnp.where(values < 0.0, tail, 1.0 - tail)
+    return values * below, below + values * decay * 0.3989422804014327
+
+
+def norm_rows(total, source, gain, normed, inverse):
+    width = gain.shape[-1]
+
+    def body(chunk):
+        rows = pl.ds(pl.multiple_of(chunk * CHUNK, CHUNK), CHUNK)
+        stream = source[rows, :].astype(F32)
+        centered = stream - jnp.sum(stream, axis=-1, keepdims=True) * (1.0 / width)
+        scale = lax.rsqrt(jnp.sum(centered * centered, axis=-1, keepdims=True) * (1.0 / width) + eps)
+        inverse[rows, :] = scale
+        normed[rows, :] = (centered * scale * gain).astype(BF)
+
+    each(total // CHUNK, body)
+
+
+def norm_back(total, grad_normed, normed, inverse, gain, added, emit, partial):
+    width = gain.shape[-1]
+    over = 1.0 / gain
+    partial[...] = jnp.zeros_like(partial)
+
+    def body(chunk):
+        rows = pl.ds(pl.multiple_of(chunk * CHUNK, CHUNK), CHUNK)
+        grad = grad_normed[rows, :]
+        unit = normed[rows, :].astype(F32)
+        both = grad * unit
+        scaled = grad * gain
+        first = jnp.sum(scaled, axis=-1, keepdims=True) * (1.0 / width)
+        second = jnp.sum(both, axis=-1, keepdims=True) * (1.0 / width)
+        emit(rows, inverse[rows, :] * (scaled - first - unit * over * second) + added[rows, :].astype(F32))
+        partial[...] += jnp.sum(both.reshape(CHUNK // 8, 8, width), axis=0)
+
+    each(total // CHUNK, body)
+    return jnp.sum(partial[...], axis=0, keepdims=True) * over
+
+
+def head_masks(size):
+    lane = lax.broadcasted_iota(jnp.int32, (1, LANES), 1)
+    return [((lane >= h * size) & (lane < (h + 1) * size)).astype(F32) for h in range(LANES // size)]
+
+
+def split_heads(block, masks):
+    return jnp.concatenate([block * mask.astype(BF) for mask in masks], axis=0)
+
+
+def merge_heads(stacked, masks, rows):
+    total = stacked[:rows] * masks[0]
+    for h in range(1, len(masks)):
+        total = total + stacked[h * rows : (h + 1) * rows] * masks[h]
+    return total
+
+
+def attend_block(packed, width, rows, size, image, group, limit, kept, mixed):
+    masks = head_masks(size)
+    heads = len(masks)
+    at = pl.ds(pl.multiple_of(image * rows, 16), rows)
+    queries = packed[at, group * LANES : (group + 1) * LANES]
+    keys = packed[at, width + group * LANES : width + (group + 1) * LANES]
+    values = packed[at, 2 * width + group * LANES : 2 * width + (group + 1) * LANES]
+    scores = (nt(split_heads(keys, masks), queries) * size**-0.5).reshape(heads, rows, rows)
+    live = lax.broadcasted_iota(jnp.int32, (1, rows, 1), 1) < limit
+    scores = jnp.where(live, scores, -1e30)
+    raised = jnp.exp(scores - jnp.max(scores, axis=1, keepdims=True))
+    weights = raised * (1.0 / jnp.sum(raised, axis=1, keepdims=True))
+    low = weights.reshape(heads * rows, rows).astype(BF)
+    kept[image, group] = low
+    mixed[at, group * LANES : (group + 1) * LANES] = tn(low, split_heads(values, masks)).astype(BF)
+
+
+def attend_back_block(packed, width, rows, size, image, group, kept, grad_mixed, grad_packed):
+    masks = head_masks(size)
+    heads = len(masks)
+    at = pl.ds(pl.multiple_of(image * rows, 16), rows)
+    queries = packed[at, group * LANES : (group + 1) * LANES]
+    keys = packed[at, width + group * LANES : width + (group + 1) * LANES]
+    values = packed[at, 2 * width + group * LANES : 2 * width + (group + 1) * LANES]
+    grad_out = grad_mixed[at, group * LANES : (group + 1) * LANES]
+    low = kept[image, group]
+    weights = low.astype(F32)
+    both = weights * nt(split_heads(values, masks), grad_out)
+    inner = jnp.sum(both.reshape(heads, rows, rows), axis=1, keepdims=True)
+    grad_scores = both - (weights.reshape(heads, rows, rows) * inner).reshape(heads * rows, rows)
+    grad_scores = grad_scores.astype(BF)
+    grad_values = merge_heads(nn(low, grad_out), masks, rows)
+    grad_keys = merge_heads(nn(grad_scores, queries), masks, rows) * size**-0.5
+    grad_queries = tn(grad_scores, split_heads(keys, masks)) * size**-0.5
+    grad_packed[at, group * LANES : (group + 1) * LANES] = grad_queries.astype(BF)
+    grad_packed[at, width + group * LANES : width + (group + 1) * LANES] = grad_keys.astype(BF)
+    grad_packed[at, 2 * width + group * LANES : 2 * width + (group + 1) * LANES] = grad_values.astype(BF)
+
+
+def pad_images(source, target, rows):
+    images, count = source.shape[0], source.shape[1]
+    whole = count // 16 * 16
+    for image in range(images):
+        target[image * rows + whole : (image + 1) * rows, :] = jnp.zeros((rows - whole, target.shape[1]), target.dtype)
+        target[image * rows : image * rows + count, :] = source[image]
+
+
+def enc_forward_kernel(
+    rows, counts, stream, gain_one, qkv, out, gain_two, up, down,
+    normed_one, inverse_one, packed, kept, mixed, normed_two, inverse_two, active, slope, encoded,
+    padded_in, middle,
+):
+    images = stream.shape[0]
+    total = images * rows
+    width = stream.shape[-1]
+    pad_images(stream, padded_in, rows)
+    norm_rows(total, padded_in, gain_one[...].astype(F32), normed_one, inverse_one)
+
+    def project(tile):
+        packed[:, columns(tile)] = nn(normed_one[...], qkv[:, columns(tile)]).astype(BF)
+
+    each(qkv.shape[1] // TILE, project)
+
+    def mix(image):
+        for group in range(width // LANES):
+            attend_block(packed, width, rows, width // HEADS, image, group, counts[image], kept, mixed)
+
+    each(images, mix)
+
+    def add_out(tile):
+        middle[:, columns(tile)] = padded_in[:, columns(tile)].astype(F32) + nn(mixed[...], out[:, columns(tile)])
+
+    each(width // TILE, add_out)
+    norm_rows(total, middle, gain_two[...].astype(F32), normed_two, inverse_two)
+    feed_up(normed_two, up, active, slope)
+
+    def add_down(tile):
+        encoded[:, columns(tile)] = (middle[:, columns(tile)] + nn(active[...], down[:, columns(tile)])).astype(BF)
+
+    each(width // TILE, add_down)
+
+
+def feed_up(normed, up, active, slope):
+    def body(tile):
+        value, derivative = gelu_pair(nn(normed[...], up[:, columns(tile)]))
+        active[:, columns(tile)] = value.astype(BF)
+        slope[:, columns(tile)] = derivative.astype(BF)
+
+    each(up.shape[1] // TILE, body)
+
+
+def feed_back(grad_low, down, slope, grad_pre):
+    def body(tile):
+        grad = nt(grad_low[...], down[columns(tile), :]) * slope[:, columns(tile)].astype(F32)
+        grad_pre[:, columns(tile)] = grad.astype(BF)
+
+    each(down.shape[0] // TILE, body)
+
+
+def times_back(grad, matrix, result):
+    def body(tile):
+        result[:, columns(tile)] = nt(grad[...], matrix[columns(tile), :]).astype(result.dtype)
+
+    each(matrix.shape[0] // TILE, body)
+
+
+def one_hot(positions, image, limit, slots, places):
+    place = lax.broadcasted_iota(jnp.int32, (places, slots), 0)
+    slot = lax.broadcasted_iota(jnp.int32, (places, slots), 1)
+    return jnp.where((positions[image : image + 1, :slots] == place) & (slot < limit), 1.0, 0.0)
+
+
+def send_tiles(count, first, rows, gathered, place, sems, tile, slots=2):
+    def copy(slot, at):
+        return pltpu.make_async_copy(place(slot), gathered.at[:, pl.ds(at, rows), :], sems.at[slot])
+
+    def body(n):
+        slot = lax.rem(n, slots)
+
+        @pl.when(n >= slots)
+        def _():
+            copy(slot, first).wait()
+
+        place(slot)[...] = tile(n).reshape(32, rows, TILE)
+        copy(slot, pl.multiple_of(first + n * rows, 8)).start()
+
+    each(count, body)
+    for n in range(max(count - slots, 0), count):
+        copy(n % slots, first).wait()
+
+
+def dec_kernel(
+    erows, drows, counts, positions, encoded, embed, mask_token, table,
+    gain_one, qkv, out, gain_two, up, down, cotangent,
+    result, grad_encoded, grad_embedded, vectors, gathered,
+    filled, normed_one, inverse_one, packed, kept, mixed, middle, normed_two, inverse_two, active, slope,
+    grad_wide, wide, partial, stage_down, stage_up, sem_down, sem_up, sem_embed,
+):
+    images, places = cotangent.shape[0], cotangent.shape[1]
+    total = images * drows
+    width = cotangent.shape[-1]
+    high, rest = mixed, grad_wide
+    embedded_rows = images * erows
+
+    def embed_tile(tile):
+        value = nn(encoded[...], embed[:, columns(tile)])
+        top = value.astype(BF)
+        high[pl.ds(0, embedded_rows), columns(tile)] = top
+        rest[pl.ds(0, embedded_rows), columns(tile)] = (value - top.astype(F32)).astype(BF)
+
+    each(width // TILE, embed_tile)
+    row = lax.broadcasted_iota(jnp.int32, (drows, 1), 0)
+    for image in range(images):
+        pick = one_hot(positions, image, counts[image], erows, drows)
+        low_pick = pick.astype(BF)
+        slots = pl.ds(image * erows, erows)
+        picked = nn(low_pick, high[slots, :]) + nn(low_pick, rest[slots, :])
+        covered = jnp.sum(pick, axis=1, keepdims=True) > 0.5
+        value = jnp.where(covered, picked, mask_token[...].astype(F32)) + table[...]
+        filled[pl.ds(image * drows, drows), :] = jnp.where(row < places, value, 0.0).astype(BF)
+
+    norm_rows(total, filled, gain_one[...].astype(F32), normed_one, inverse_one)
+
+    def project(tile):
+        packed[:, columns(tile)] = nn(normed_one[...], qkv[:, columns(tile)]).astype(BF)
+
+    each(qkv.shape[1] // TILE, project)
+
+    def mix(image):
+        for group in range(width // LANES):
+            attend_block(packed, width, drows, width // DHEADS, image, group, places, kept, mixed)
+
+    each(images, mix)
+
+    def add_out(tile):
+        middle[:, columns(tile)] = filled[:, columns(tile)].astype(F32) + nn(mixed[...], out[:, columns(tile)])
+
+    each(width // TILE, add_out)
+    norm_rows(total, middle, gain_two[...].astype(F32), normed_two, inverse_two)
+    feed_up(normed_two, up, active, slope)
+
+    for tile in range(width // TILE):
+        at = slice(tile * TILE, (tile + 1) * TILE)
+        value = (middle[:, at] + nn(active[...], down[:, at])).astype(BF)
+        for image in range(images):
+            result[image, :, at] = value[image * drows : image * drows + places]
+
+    grad_low = grad_wide
+    pad_images(cotangent, grad_low, drows)
+    at = 0
+    block = down.shape[0] // 32
+    send_tiles(width // TILE, at, block, gathered, lambda slot: stage_down, sem_down, lambda n: tn(active[...], grad_low[:, columns(n)]), 1)
+    at += width // TILE * block
+    block = width // 32
+    feed_back(grad_low, down, slope, slope)
+    send_tiles(up.shape[1] // TILE, at, block, gathered, lambda slot: stage_up.at[slot], sem_up, lambda n: tn(normed_two[...], slope[:, columns(n)]))
+    at += up.shape[1] // TILE * block
+    times_back(slope, up, middle)
+    grad_attend = grad_wide
+
+    def keep_middle(rows, grad):
+        middle[rows, :] = grad
+        grad_attend[rows, :] = grad.astype(BF)
+
+    vectors[...] = jnp.zeros_like(vectors)
+    vectors[1:2, :] = norm_back(total, middle, normed_two, inverse_two, gain_two[...].astype(F32), grad_low, keep_middle, partial)
+    send_tiles(width // TILE, at, block, gathered, lambda slot: stage_up.at[slot], sem_up, lambda n: tn(mixed[...], grad_attend[:, columns(n)]))
+    at += width // TILE * block
+    grad_mixed = normed_two
+    times_back(grad_attend, out, grad_mixed)
+
+    def mix_back(image):
+        for group in range(width // LANES):
+            attend_back_block(packed, width, drows, width // DHEADS, image, group, kept, grad_mixed, packed)
+
+    each(images, mix_back)
+    send_tiles(qkv.shape[1] // TILE, at, block, gathered, lambda slot: stage_up.at[slot], sem_up, lambda n: tn(normed_one[...], packed[:, columns(n)]))
+    at += qkv.shape[1] // TILE * block
+    times_back(packed, qkv, wide)
+
+    def keep_filled(rows, grad):
+        filled[rows, :] = grad.astype(BF)
+
+    vectors[0:1, :] = norm_back(total, wide, normed_one, inverse_one, gain_one[...].astype(F32), middle, keep_filled, partial)
+    token = jnp.zeros((1, width), F32)
+    for image in range(images):
+        pick = one_hot(positions, image, counts[image], erows, drows)
+        covered = jnp.sum(pick, axis=1, keepdims=True) > 0.5
+        grad = filled[pl.ds(image * drows, drows), :]
+        token = token + jnp.sum(jnp.where(covered | (row >= places), 0.0, grad.astype(F32)), axis=0, keepdims=True)
+        grad_embedded[pl.ds(image * erows, erows), :] = tn(pick.astype(BF), grad).astype(BF)
+    vectors[2:3, :] = token
+    block = embed.shape[0] // 32
+
+    def embed_place(slot):
+        return stage_down.at[:, pl.ds(pl.multiple_of(slot * block, 8), block), :]
+
+    send_tiles(width // TILE, at, block, gathered, embed_place, sem_embed, lambda n: tn(encoded[...], grad_embedded[:, columns(n)]))
+    times_back(grad_embedded, embed, grad_encoded)
+
+
+def coords():
+    seq, dp = lax.axis_index("seq"), lax.axis_index("dp")
+    return {"s": dp // 4, "l": (dp // 2) % 2, "y": dp % 2, "x": seq // 2, "c": seq % 2}
+
+
+def partner(here, dim):
+    other = dict(here)
+    other[dim] = 1 - here[dim]
+    return (other["s"] * 4 + other["l"] * 2 + other["y"], other["x"] * 2 + other["c"])
+
+
+class Reduction:
+    def __init__(self, steps, result, scratch):
+        self.steps, self.result = steps, result
+        self.stage, self.land = scratch[0], scratch[1]
+        self.lands = [scratch[2 + 4 * f : 6 + 4 * f] for f in range(4)]
+        self.send_sem, self.recv_sem = scratch[18:20]
+        self.here = coords()
+
+    @staticmethod
+    def scratch(steps):
+        shapes = [pltpu.VMEM((2, 2, 2, 2, 2, 2, STEP, TILE), F32), pltpu.VMEM((steps, 2, 2, 2, 2, STEP, TILE), F32)]
+        for _, rows, _ in FLOWS:
+            for k in range(1, 5):
+                shapes.append(pltpu.VMEM((steps,) + (2,) * (4 - k) + (rows, TILE), F32))
+        return shapes + [pltpu.SemaphoreType.DMA((steps, 17)), pltpu.SemaphoreType.DMA((steps, 17))]
+
+    def enter(self):
+        barrier = pltpu.get_barrier_semaphore()
+        for dim in "c" + DIMS:
+            pl.semaphore_signal(barrier, inc=1, device_id=partner(self.here, dim), device_id_type=MESH)
+        pl.semaphore_wait(barrier, 5)
+
+    def core_copy(self, t):
+        return pltpu.make_async_remote_copy(
+            src_ref=self.stage.at[lax.rem(t, 2), :, :, :, :, 1 - self.here["c"]],
+            dst_ref=self.land.at[t],
+            send_sem=self.send_sem.at[t, 16],
+            recv_sem=self.recv_sem.at[t, 16],
+            device_id=partner(self.here, "c"),
+            device_id_type=MESH,
+        )
+
+    def half(self, t, flow, k, kept):
+        first, rows, order = FLOWS[flow]
+        left = [dim for dim in DIMS if dim not in order[:k]]
+        side = self.here[order[k]] if kept else 1 - self.here[order[k]]
+        at = (t,) + tuple(side if dim == order[k] else slice(None) for dim in left)
+        if k == 0:
+            return self.land.at[at + (pl.ds(first, rows),)]
+        return self.lands[flow][k - 1].at[at]
+
+    def copy(self, t, flow, k):
+        return pltpu.make_async_remote_copy(
+            src_ref=self.half(t, flow, k, False),
+            dst_ref=self.lands[flow][k].at[t],
+            send_sem=self.send_sem.at[t, flow * 4 + k],
+            recv_sem=self.recv_sem.at[t, flow * 4 + k],
+            device_id=partner(self.here, FLOWS[flow][2][k]),
+            device_id_type=MESH,
+        )
+
+    def advance(self, k, t):
+        if k == 1:
+            self.core_copy(t).wait()
+            self.land[t] += self.stage[lax.rem(t, 2), :, :, :, :, self.here["c"]]
+            for flow in range(4):
+                self.copy(t, flow, 0).start()
+            return
+        for flow in range(4):
+            self.copy(t, flow, k - 2).wait()
+            kept = self.half(t, flow, k - 2, True)
+            if k < 5:
+                self.lands[flow][k - 2][t] += kept[...]
+                self.copy(t, flow, k - 1).start()
+            else:
+                first, rows, _ = FLOWS[flow]
+                at = pl.ds(pl.multiple_of(t * STEP + first, 8), rows)
+                self.result[at, :] = self.lands[flow][3][t] + kept[...]
+
+    def step(self, t, fill=None):
+        if fill is not None:
+            fill(t)
+            self.core_copy(t).start()
+        for k in range(1, 6):
+            @pl.when((t >= k) & (t < self.steps + k))
+            def _():
+                self.advance(k, t - k)
+
+
+def staged_load(reduction, gathered, sems):
+    def load(t):
+        rows = pl.ds(pl.multiple_of(t * STEP, 8), STEP)
+        return pltpu.make_async_copy(gathered.at[:, :, :, :, :, rows, :], reduction.stage.at[lax.rem(t, 2)], sems.at[lax.rem(t, 2)])
+
+    return load
+
+
+def enc_back_kernel(
+    rows, steps,
+    grad_encoded, active, slope, normed_two, inverse_two, gain_two, packed, kept, normed_one, inverse_one, gain_one,
+    qkv, out, up, down, gathered,
+    grad_low, grad_pre, grad_attend, grad_packed, input_grad, vectors, gathered_down, reduced,
+    middle, wide, grad_mixed, partial, stage_down, weight, sem_down, sem_in, sem_load, *scratch,
+):
+    images, slots = input_grad.shape[0], input_grad.shape[1]
+    total = images * rows
+    width = middle.shape[-1]
+    reduction = Reduction(steps, reduced, scratch)
+    load = staged_load(reduction, gathered, sem_load)
+    into_pre = pltpu.make_async_copy(slope, grad_pre, sem_in.at[0])
+    into_packed = pltpu.make_async_copy(packed, grad_packed, sem_in.at[1])
+    into_wide = pltpu.make_async_copy(grad_encoded, wide, sem_in.at[2])
+    into_up = pltpu.make_async_copy(up, weight, sem_in.at[3])
+    into_qkv = pltpu.make_async_copy(qkv, weight.at[:, : qkv.shape[1]], sem_in.at[4])
+    into_wide.start()
+    into_pre.start()
+    load(0).start()
+    into_packed.start()
+    into_up.start()
+    reduction.enter()
+
+    def communicate(t):
+        load(t).wait()
+        reduction.step(t, lambda _: None)
+
+        @pl.when(t + 1 < steps)
+        def _():
+            load(t + 1).start()
+
+    def low_chunk(chunk):
+        at = pl.ds(pl.multiple_of(chunk * CHUNK, CHUNK), CHUNK)
+        grad_low[at, :] = wide[at, :].astype(BF)
+
+    into_wide.wait()
+    each(total // CHUNK, low_chunk)
+    into_pre.wait()
+    block = down.shape[0] // 32
+
+    def down_tile(n):
+        return tn(active[...], grad_low[:, columns(n)])
+
+    def copy_down(n):
+        return pltpu.make_async_copy(stage_down.at[0], gathered_down.at[:, pl.ds(pl.multiple_of(n * block, 8), block), :], sem_down.at[0])
+
+    def send_down(n):
+        @pl.when(n > 0)
+        def _():
+            copy_down(n - 1).wait()
+
+        stage_down[0] = down_tile(n).reshape(stage_down.shape[1:])
+        copy_down(n).start()
+        communicate(n)
+
+    each(width // TILE, send_down)
+    copy_down(width // TILE - 1).wait()
+    feed_back(grad_low, down, grad_pre, grad_pre)
+    into_up.wait()
+    times_back(grad_pre, weight, middle)
+    into_qkv.start()
+
+    def keep_middle(at, grad):
+        middle[at, :] = grad
+        grad_attend[at, :] = grad.astype(BF)
+
+    vectors[...] = jnp.zeros_like(vectors)
+    vectors[1:2, :] = norm_back(total, middle, normed_two, inverse_two, gain_two[...].astype(F32), wide, keep_middle, partial)
+    times_back(grad_attend, out, grad_mixed)
+    into_packed.wait()
+    first = width // TILE
+
+    def mix_back(image):
+        for group in range(width // LANES):
+            attend_back_block(grad_packed, width, rows, width // HEADS, image, group, kept, grad_mixed, grad_packed)
+
+        @pl.when(first + image < steps)
+        def _():
+            communicate(first + image)
+
+    each(images, mix_back)
+    into_qkv.wait()
+    times_back(grad_packed, weight.at[:, : qkv.shape[1]], wide)
+
+    def keep_input(at, grad):
+        wide[at, :] = grad
+
+    vectors[0:1, :] = norm_back(total, wide, normed_one, inverse_one, gain_one[...].astype(F32), middle, keep_input, partial)
+    for image in range(images):
+        input_grad[image] = wide[image * rows : image * rows + slots, :]
+    each(5, lambda k: reduction.step(steps + k))
+
+
+def enc_weights_kernel(
+    steps,
+    normed_two, grad_pre, mixed, grad_attend, normed_one, grad_packed, gathered_down, vector,
+    reduced, vector_sum,
+    vector_part, vector_land, vector_send, vector_recv, sem_load, *scratch,
+):
+    reduction = Reduction(steps, reduced, scratch)
+    load = staged_load(reduction, gathered_down, sem_load)
+    ready = gathered_down.shape[-2] // STEP
+    load(0).start()
+    reduction.enter()
+    order = "c" + DIMS
+
+    def vector_copy(k):
+        return pltpu.make_async_remote_copy(
+            src_ref=vector_part.at[k],
+            dst_ref=vector_land.at[k],
+            send_sem=vector_send.at[k],
+            recv_sem=vector_recv.at[k],
+            device_id=partner(reduction.here, order[k]),
+            device_id_type=MESH,
+        )
+
+    def vector_step(t):
+        for k in range(6):
+            @pl.when(t == k)
+            def _():
+                if k == 0:
+                    vector_part[0] = vector[...]
+                else:
+                    vector_copy(k - 1).wait()
+                    vector_part[k] = vector_part[k - 1] + vector_land[k - 1]
+                if k < 5:
+                    vector_copy(k).start()
+
+    def from_memory(t):
+        load(t).wait()
+        reduction.step(t, lambda _: None)
+        vector_step(t)
+
+        @pl.when(t + 1 < ready)
+        def _():
+            load(t + 1).start()
+
+    each(ready, from_memory)
+
+    def from_product(first, left, right):
+        block = left.shape[1] // 32
+        count = STEP // block
+
+        def fill(t):
+            for i in range(count):
+                tile = tn(left[...], right[:, columns((t - first) * count + i)])
+                reduction.stage[lax.rem(t, 2), :, :, :, :, :, i * block : (i + 1) * block, :] = tile.reshape(2, 2, 2, 2, 2, block, TILE)
+
+        def body(s):
+            reduction.step(first + s, fill)
+            vector_step(first + s)
+
+        number = right.shape[1] // TILE // count
+        each(number, body)
+        return first + number
+
+    at = from_product(ready, normed_two, grad_pre)
+    at = from_product(at, normed_one, grad_packed)
+    at = from_product(at, mixed, grad_attend)
+    each(5, lambda k: reduction.step(steps + k))
+    here = reduction.here
+    index = (here["s"] * 4 + here["l"] * 2 + here["y"]) * 4 + here["x"] * 2 + here["c"]
+    vector_sum[...] = vector_part[5, pl.ds(index, 1), :]
+
+
+def unpack_kernel(layout, *refs):
+    sources, targets = refs[:2], refs[2:]
+    at = [0, 0]
+    for (which, _), target in zip(layout, targets):
+        block, width = target.shape
+        for n in range(width // TILE):
+            target[:, n * TILE : (n + 1) * TILE] = sources[which][at[which] : at[which] + block, :]
+            at[which] += block
+
+
+def vmem(count):
+    return [pl.BlockSpec(memory_space=pltpu.VMEM)] * count
+
+
+def anywhere(count):
+    return [pl.BlockSpec(memory_space=pl.ANY)] * count
+
+
+def shapes(*pairs):
+    return [jax.ShapeDtypeStruct(shape, dtype) for shape, dtype in pairs]
+
+
+def scratches(*pairs):
+    return [pltpu.VMEM(shape, dtype) for shape, dtype in pairs]
+
+
+def cost(flops, bytes_accessed):
+    return pl.CostEstimate(flops=flops, bytes_accessed=bytes_accessed, transcendentals=0)
+
+
+def fast_local(
+    enc_input, keep_count, keep_positions,
+    enc_gain_one, enc_qkv_weight, enc_out_weight, enc_gain_two, enc_up_weight, enc_down_weight,
+    embed_weight, mask_token,
+    dec_gain_one, dec_qkv_weight, dec_out_weight, dec_gain_two, dec_up_weight, dec_down_weight,
+    cotangent,
+):
+    images, slots, width = enc_input.shape
+    places, dwidth = cotangent.shape[1:]
+    hidden, dhidden = enc_up_weight.shape[1], dec_up_weight.shape[1]
+    erows, drows = padded(slots, 16), padded(places, 16)
+    etotal, dtotal = images * erows, images * drows
+    egroups, dgroups = width // LANES, dwidth // LANES
+    eheads, dheads = HEADS // egroups, DHEADS // dgroups
+    smem = [pl.BlockSpec(memory_space=pltpu.SMEM)]
+    settings = functools.partial(pltpu.CompilerParams, vmem_limit_bytes=VMEM_BYTES)
+    row = lambda vector: vector.reshape(1, -1)
+
+    normed_one, inverse_one, packed, kept, mixed, normed_two, inverse_two, active, slope, encoded = pl.pallas_call(
+        functools.partial(enc_forward_kernel, erows),
+        name="enc_forward",
+        out_shape=shapes(
+            ((etotal, width), BF), ((etotal, 1), F32), ((etotal, 3 * width), BF), ((images, egroups, eheads * erows, erows), BF),
+            ((etotal, width), BF), ((etotal, width), BF), ((etotal, 1), F32), ((etotal, hidden), BF), ((etotal, hidden), BF), ((etotal, width), BF),
+        ),
+        in_specs=smem + vmem(7),
+        out_specs=vmem(10),
+        scratch_shapes=scratches(((etotal, width), BF), ((etotal, width), F32)),
+        compiler_params=settings(),
+    )(keep_count, enc_input, row(enc_gain_one), enc_qkv_weight, enc_out_weight, row(enc_gain_two), enc_up_weight, enc_down_weight)
+
+    table = jnp.asarray(position_rows(places, dwidth, drows))
+    block_down, block, block_embed = dhidden // 32, dwidth // 32, width // 32
+    dec_rows = dwidth // TILE * (block_down + block + block_embed) + (dhidden + 3 * dwidth) // TILE * block
+    dec_output, grad_encoded, grad_embedded, dec_vectors, gathered = pl.pallas_call(
+        functools.partial(dec_kernel, erows, drows),
+        name="decoder",
+        out_shape=shapes(
+            (cotangent.shape, BF), ((etotal, width), F32), ((etotal, dwidth), BF), ((8, dwidth), F32), ((32, dec_rows, TILE), F32),
+        ),
+        in_specs=smem + vmem(12),
+        out_specs=vmem(4) + anywhere(1),
+        scratch_shapes=scratches(
+            ((dtotal, dwidth), BF), ((dtotal, dwidth), BF), ((dtotal, 1), F32), ((dtotal, 3 * dwidth), BF),
+            ((images, dgroups, dheads * drows, drows), BF), ((dtotal, dwidth), BF), ((dtotal, dwidth), F32), ((dtotal, dwidth), BF),
+            ((dtotal, 1), F32), ((dtotal, dhidden), BF), ((dtotal, dhidden), BF), ((dtotal, dwidth), BF), ((dtotal, dwidth), F32),
+            ((8, dwidth), F32), ((32, block_down, TILE), F32), ((2, 32, block, TILE), F32),
+        ) + [pltpu.SemaphoreType.DMA((2,))] * 3,
+        compiler_params=settings(),
+    )(
+        keep_count, jnp.pad(keep_positions, ((0, 0), (0, erows - slots))), encoded, embed_weight, row(mask_token), table,
+        row(dec_gain_one), dec_qkv_weight, dec_out_weight, row(dec_gain_two), dec_up_weight, dec_down_weight, cotangent,
+    )
+
+    dec_steps = dec_rows // STEP
+    down_rows = width // TILE * (hidden // 32)
+    grad_low, grad_pre, grad_attend, grad_packed, input_grad, enc_vectors, gathered_down, dec_reduced = pl.pallas_call(
+        functools.partial(enc_back_kernel, erows, dec_steps),
+        name="enc_back",
+        out_shape=shapes(
+            ((etotal, width), BF), ((etotal, hidden), BF), ((etotal, width), BF), ((etotal, 3 * width), BF),
+            (enc_input.shape, F32), ((8, width), F32), ((32, down_rows, TILE), F32), ((dec_rows, TILE), F32),
+        ),
+        in_specs=anywhere(1) + vmem(1) + anywhere(1) + vmem(3) + anywhere(1) + vmem(4) + anywhere(1) + vmem(1) + anywhere(1) + vmem(1) + anywhere(1),
+        out_specs=vmem(6) + anywhere(1) + vmem(1),
+        scratch_shapes=scratches(
+            ((etotal, width), F32), ((etotal, width), F32), ((etotal, width), BF), ((8, width), F32), ((1, 32, hidden // 32, TILE), F32), (enc_up_weight.shape, BF),
+        ) + [pltpu.SemaphoreType.DMA((1,)), pltpu.SemaphoreType.DMA((5,)), pltpu.SemaphoreType.DMA((2,))] + Reduction.scratch(dec_steps),
+        compiler_params=settings(collective_id=0, has_side_effects=True),
+    )(
+        grad_encoded, active, slope, normed_two, inverse_two, row(enc_gain_two), packed, kept, normed_one, inverse_one, row(enc_gain_one),
+        enc_qkv_weight, enc_out_weight, enc_up_weight, enc_down_weight, gathered.reshape(2, 2, 2, 2, 2, dec_rows, TILE),
+    )
+
+    share = lambda vector: vector.reshape(32, -1)
+    vector = jnp.concatenate(
+        [share(enc_vectors[0]), share(enc_vectors[1]), share(dec_vectors[2]), share(dec_vectors[0]), share(dec_vectors[1])], axis=1
+    )
+    vector = jnp.pad(vector, ((0, 0), (0, LANES - vector.shape[1])))
+    enc_rows = down_rows + (hidden + 4 * width) // TILE * block_embed
+    enc_steps = enc_rows // STEP
+    enc_reduced, vector_sum = pl.pallas_call(
+        functools.partial(enc_weights_kernel, enc_steps),
+        name="enc_weights",
+        out_shape=shapes(((enc_rows, TILE), F32), ((1, LANES), F32)),
+        in_specs=vmem(6) + anywhere(1) + vmem(1),
+        out_specs=vmem(2),
+        scratch_shapes=scratches(((6, 32, LANES), F32), ((5, 32, LANES), F32))
+        + [pltpu.SemaphoreType.DMA((5,)), pltpu.SemaphoreType.DMA((5,)), pltpu.SemaphoreType.DMA((2,))]
+        + Reduction.scratch(enc_steps),
+        compiler_params=settings(collective_id=1, has_side_effects=True),
+    )(normed_two, grad_pre, mixed, grad_attend, normed_one, grad_packed, gathered_down.reshape(2, 2, 2, 2, 2, down_rows, TILE), vector)
+
+    layout = (
+        (0, (block_down, dwidth)), (0, (block, dhidden)), (0, (block, dwidth)), (0, (block, 3 * dwidth)), (0, (block_embed, dwidth)),
+        (1, (hidden // 32, width)), (1, (block_embed, hidden)), (1, (block_embed, 3 * width)), (1, (block_embed, width)),
+    )
+    dec_down, dec_up, dec_out, dec_qkv, embed, enc_down, enc_up, enc_qkv, enc_out = pl.pallas_call(
+        functools.partial(unpack_kernel, layout),
+        name="unpack",
+        out_shape=shapes(*((shape, F32) for _, shape in layout)),
+        in_specs=vmem(2),
+        out_specs=vmem(9),
+    )(dec_reduced, enc_reduced)
+    cuts = []
+    at = 0
+    for size in (width // 32, width // 32, dwidth // 32, dwidth // 32, dwidth // 32):
+        cuts.append(vector_sum[0, at : at + size])
+        at += size
+    return (
+        dec_output, input_grad, cuts[0], enc_qkv, enc_out, cuts[1], enc_up, enc_down, embed, cuts[2],
+        cuts[3], dec_qkv, dec_out, cuts[4], dec_up, dec_down,
+    )
+
+
+def position_rows(places, width, rows):
+    side = math.isqrt(places)
+    quarter = width // 4
+    place = np.arange(places)
+    rate = 1.0 / 10000.0 ** (np.arange(quarter) / quarter)
+    across, down = place[:, None] % side * rate, place[:, None] // side * rate
+    table = np.concatenate([np.sin(across), np.cos(across), np.sin(down), np.cos(down)], axis=1)
+    return np.pad(table, ((0, rows - places), (0, 0))).astype(np.float32)
+
+
 def solution(mesh):
     placed = (
         P(("dp", "seq"), None, None),
@@ -400,8 +1144,9 @@
         P(),
         P(("dp", "seq"), None, None),
     )
+    fast = (mesh.shape["dp"], mesh.shape["seq"]) == (8, 4)
     return jax.shard_map(
-        local,
+        fast_local if fast else local,
         mesh=mesh,
         in_specs=placed,
         out_specs=(

time: 1850 us -> 371 us (0.20)
  waiting for transfers between devices: 1090 us -> 0 us
  matrix products: 541 us -> 0 us
  Pallas kernels: 0 us -> 358 us
  local copies, waits for them, and re-layouts: 82.8 us -> 11.5 us
  other arithmetic: 70.3 us -> 0 us
  blocking collectives: 42.2 us -> 0 us
    reduce_scatter x9 -> x0, waiting for transfers between devices: 1080 us -> none  [the longest x1 142 us: local(): lax.psum_scatter(totals[4], ('dp', 'seq'), scatter_dimension=0, tiled=True)]
    dot_general x222 -> x0, matrix products: 515 us -> none  [the longest x54 209 us: outer_sum(): lax.dot_general(flat_left, flat_right, (((0,), (0,)), ((), ())), preferre...]
    pallas_call x0 -> x5, Pallas kernels: none -> 358 us  [the longest x1 123 us: fast_local(): pl.pallas_call(functools.partial(enc_weights_kernel, enc_steps), name='en...]
    while x1212 -> x0, local copies, waits for them, and re-layouts: 49.8 us -> none
    unnamed x1 -> x0, blocking collectives: 42.2 us -> none
    sub x12 -> x0, matrix products: 26.2 us -> none  [attend(): raised = jnp.exp(scores - row_max)]
    reduce_sum x48 -> x0, other arithmetic: 24.7 us -> none  [the longest x24 10.3 us: layer_norm(): jnp.mean(centered * centered, axis=-1, keepdims=True) + eps]
  transfers between devices with their start and end apart: 9 -> 0, of which waited for: 9 -> 0; matrix products, arithmetic and copies ran while one was open for 0% -> 0% of each run, Pallas kernels for 0% -> 0%
where the time goes in v2:
time: 371 us; the launch traced here: 370 us
  Pallas kernels  358 us (96%)
  local copies, waits for them, and re-layouts  11.5 us (3%)
    pallas_call x1, Pallas kernels, fast_local(): pl.pallas_call(functools.partial(enc_weights_kernel, enc_steps), name='en...  123 us
    pallas_call x1, Pallas kernels, fast_local(): pl.pallas_call(functools.partial(dec_kernel, erows, drows), name='decoder...  100 us
    pallas_call x1, Pallas kernels, fast_local(): pl.pallas_call(functools.partial(enc_back_kernel, erows, dec_steps), name...  92.6 us
    pallas_call x1, Pallas kernels, fast_local(): pl.pallas_call(functools.partial(enc_forward_kernel, erows), name='enc_fo...  39.9 us

profile of v2, /device:TPU:0, one launch (start us, length us, event | category | flops | bytes accessed | tf_op | source)
XLA Modules:
  0.0 370.4 jit_solution(12002307255981893868)
XLA Ops:
  0.6 1.3 reshape.55.gain_one
  1.9 1.3 reshape.56.gain_two
  3.2 0.0 copy-start.1
  3.2 0.0 copy-start.3
  3.2 0.0 copy-start.4
  3.2 39.9 %enc_forward.1 = (bf16[672,768]{1,0:T(8,128)(2,1)}, f32[672,1]{1,0:T(8,128)}, bf16[672,2304]{1,0:T(8,128)(2,1)}, bf16[6,6,224,112]{3,2,1,0:T(8,128)(2,1)}, bf16[...) custom-call(s32[6]{0:T(128)} %counts.3, ...), custom_call_target="tpu_custom_call" | custom-call | tf_op jit(solution)/shard_map/enc_forward/pallas_call | solution.py:1019
  43.1 0.0 copy-done.1
  43.1 0.6 pad.8.positions
  43.7 0.0 copy-done.2
  43.7 0.6 reshape.57.mask_token
  44.3 0.0 copy-done.3
  44.3 0.6 reshape.58.gain_one
  44.9 0.0 copy-done.4
  44.9 0.6 reshape.59.gain_two
  45.5 100.3 %decoder.1 = (bf16[6,196,512]{2,1,0:T(8,128)(2,1)}, f32[672,768]{1,0:T(8,128)}, bf16[672,512]{1,0:T(8,128)(2,1)}, f32[8,512]{1,0:T(8,128)}, f32[32,432,256]{2,1,0:T(8,128)}) custom-call(s32[6]{0:T(128)} %counts.3, s32[6,112]{1,0:T(8,128)} %pad.8.positions, bf16[672,768]{1,0:T(8,128)(2,1)} %get-tuple-element.48.encoded, bf16[768,512]{1,0:T(8,128)(2,1)} %embed.1, ...), custom_call_target="tpu_custom_call" | custom-call | tf_op jit(solution)/shard_map/decoder/pallas_call | solution.py:1035
  145.8 92.6 %enc_back.1 = (bf16[672,768]{1,0:T(8,128)(2,1)}, bf16[672,3072]{1,0:T(8,128)(2,1)}, bf16[672,768]{1,0:T(8,128)(2,1)}, bf16[672,2304]{1,0:T(8,128)(2,1)}, f32[6,9...) custom-call(f32[672,768]{1,0:T(8,128)} %get-tuple-element.50.grad_encoded, ...), custom_call_target="tpu_custom_call" | custom-call | tf_op jit(solution)/shard_map/enc_back/pallas_call | solution.py:1057
  238.4 0.8 slice_reduce_fusion
  239.3 0.1 reshape_squeeze.15
  239.4 0.1 reshape_squeeze.16
  239.4 0.9 slice_reduce_fusion.2
  240.3 0.1 reshape_squeeze.17
  240.4 0.1 reshape_squeeze.18
  240.5 0.1 reshape_squeeze.19
  240.5 0.1 concatenate.3
  240.6 0.6 pad.9.vector
  241.3 0.0 copy-start
  241.3 123.0 %enc_weights.1 = (f32[864,256]{1,0:T(8,128)}, f32[1,128]{1,0:T(1,128)}) custom-call(bf16[672,768]{1,0:T(8,128)(2,1)} %get-tuple-element.53.normed_two, bf16[672,3072]{1,0:T(8,128)(2,1)} %get-tuple-element.61.grad_pre, bf16[672,768]{1,0:T(8,128)(2,1)} %get-tuple-element.62.mixed, bf16[672,768]{1,0:T(8,128)(2,1)} %get-tuple-element.63.grad_attend, ...), custom_call_target="tpu_custom_call" | custom-call | tf_op jit(solution)/shard_map/enc_weights/pallas_call | solution.py:1082
  364.3 2.4 unpack.1
  366.6 1.3 slice_bitcast_fusion
  367.9 1.3 slice_bitcast_fusion.3
  369.2 0.0 copy-done
  369.2 1.3 copy.36
  (1 shorter events, 0.0 us)
Async XLA Ops:
  3.2 39.9 %copy-start.1 = (s32[6,98]{1,0:T(8,128)S(1)}, s32[6,98]{1,0:T(8,128)}, u32[]{:S(2)}) copy-start(s32[6,98]{1,0:T(8,128)} %param.21) | copy-start | bytes 7060
  3.2 40.5 %copy-start.2 = (bf16[512]{0:T(512)(128)(2,1)S(1)}, bf16[512]{0:T(512)(128)(2,1)}, u32[]{:S(2)}) copy-start(bf16[512]{0:T(512)(128)(2,1)} %param.29) | copy-start | bytes 3076
  3.2 41.1 %copy-start.3 = (bf16[512]{0:T(512)(128)(2,1)S(1)}, bf16[512]{0:T(512)(128)(2,1)}, u32[]{:S(2)}) copy-start(bf16[512]{0:T(512)(128)(2,1)} %param.30) | copy-start | bytes 3076
  3.2 41.7 %copy-start.4 = (bf16[512]{0:T(512)(128)(2,1)S(1)}, bf16[512]{0:T(512)(128)(2,1)}, u32[]{:S(2)}) copy-start(bf16[512]{0:T(512)(128)(2,1)} %param.33) | copy-start | bytes 3076
  241.3 127.9 %copy-start = (f32[6,98,768]{2,1,0:T(8,128)S(1)}, f32[6,98,768]{2,1,0:T(8,128)}, u32[]{:S(2)}) copy-start(f32[6,98,768]{2,1,0:T(8,128)} %get-tuple-element.107) | copy-start | bytes 5419012

commit v3 on v0

--- a/solution.py
+++ b/solution.py
@@ -1,8 +1,12 @@
+import functools
 import math
 
 import jax
 import jax.numpy as jnp
+import numpy as np
 from jax import lax
+from jax.experimental import pallas as pl
+from jax.experimental.pallas import tpu as pltpu
 from jax.sharding import PartitionSpec as P
 
 HEADS = 12
@@ -319,27 +323,8 @@
         dec_up_weight,
         dec_down_weight,
     )
-    totals = tuple((jnp.zeros(param.shape, jnp.float32) for param in all_params))
-
-    def one_micro(running, pieces):
-        enc_rows, counts, positions, cot_rows = pieces
-        dec_piece, grad_input, terms = micro_step(
-            enc_rows,
-            counts,
-            positions,
-            cot_rows,
-            enc_weights,
-            embed_weight,
-            mask_token,
-            dec_weights,
-        )
-        running = tuple((total + term for total, term in zip(running, terms)))
-        return (running, (dec_piece, grad_input))
-
-    totals, (dec_pieces, input_grads) = lax.scan(
-        one_micro,
-        totals,
-        (enc_input[:, None], keep_count[:, None], keep_positions[:, None], cotangent[:, None]),
+    dec_pieces, input_grads, totals = micro_step(
+        enc_input, keep_count, keep_positions, cotangent, enc_weights, embed_weight, mask_token, dec_weights
     )
     totals = (
         lax.psum_scatter(totals[0], ("dp", "seq"), scatter_dimension=0, tiled=True),
@@ -379,6 +364,815 @@
     )
 
 
+MESH = pl.DeviceIdType.MESH
+BF = jnp.bfloat16
+F32 = jnp.float32
+LANES = 128
+TILE = 256
+CHUNK = 48
+VMEM_BYTES = 62 * 2**20
+STEP = 40
+FLOWS = ((0, 16, "xyls"), (16, 16, "yxls"), (32, 8, "lsxy"))
+COPIES = 4 * len(FLOWS) + 1
+SLOTS = 7
+DIMS = "slyx"
+
+
+def padded(count, multiple):
+    return -(-count // multiple) * multiple
+
+
+def nn(left, right):
+    return lax.dot_general(left, right, (((1,), (0,)), ((), ())), preferred_element_type=F32)
+
+
+def nt(left, right):
+    return lax.dot_general(left, right, (((1,), (1,)), ((), ())), preferred_element_type=F32)
+
+
+def tn(left, right):
+    return lax.dot_general(left, right, (((0,), (0,)), ((), ())), preferred_element_type=F32)
+
+
+def columns(tile):
+    return pl.ds(pl.multiple_of(tile * TILE, TILE), TILE)
+
+
+def each(count, body):
+    lax.fori_loop(0, count, lambda index, carry: (body(index), carry)[1], 0)
+
+
+def gelu_pair(values):
+    reach = jnp.abs(values)
+    point = 1.0 / (1.0 + 0.23164189 * reach)
+    decay = jnp.exp(-0.5 * values * values)
+    tail = 0.5307027145 * point - 0.7265760135
+    tail = tail * point + 0.710706870
+    tail = tail * point - 0.142248368
+    tail = tail * point + 0.127414796
+    tail = tail * point * decay
+    below = jnp.where(values < 0.0, tail, 1.0 - tail)
+    return values * below, below + values * decay * 0.3989422804014327
+
+
+def norm_rows(total, source, gain, normed, inverse):
+    width = gain.shape[-1]
+
+    def body(chunk):
+        rows = pl.ds(pl.multiple_of(chunk * CHUNK, CHUNK), CHUNK)
+        stream = source[rows, :].astype(F32)
+        centered = stream - jnp.sum(stream, axis=-1, keepdims=True) * (1.0 / width)
+        scale = lax.rsqrt(jnp.sum(centered * centered, axis=-1, keepdims=True) * (1.0 / width) + eps)
+        inverse[rows, :] = scale
+        normed[rows, :] = (centered * scale * gain).astype(BF)
+
+    each(total // CHUNK, body)
+
+
+def norm_back(total, grad_normed, normed, inverse, gain, added, emit, partial):
+    width = gain.shape[-1]
+    over = 1.0 / gain
+    partial[...] = jnp.zeros_like(partial)
+
+    def body(chunk):
+        rows = pl.ds(pl.multiple_of(chunk * CHUNK, CHUNK), CHUNK)
+        grad = grad_normed[rows, :]
+        unit = normed[rows, :].astype(F32)
+        both = grad * unit
+        scaled = grad * gain
+        first = jnp.sum(scaled, axis=-1, keepdims=True) * (1.0 / width)
+        second = jnp.sum(both, axis=-1, keepdims=True) * (1.0 / width)
+        emit(rows, inverse[rows, :] * (scaled - first - unit * over * second) + added[rows, :].astype(F32))
+        partial[...] += jnp.sum(both.reshape(CHUNK // 8, 8, width), axis=0)
+
+    each(total // CHUNK, body)
+    return jnp.sum(partial[...], axis=0, keepdims=True) * over
+
+
+def head_masks(size):
+    lane = lax.broadcasted_iota(jnp.int32, (1, LANES), 1)
+    return [((lane >= h * size) & (lane < (h + 1) * size)).astype(F32) for h in range(LANES // size)]
+
+
+def split_heads(block, masks):
+    return jnp.concatenate([block * mask.astype(BF) for mask in masks], axis=0)
+
+
+def merge_heads(stacked, masks, rows):
+    total = stacked[:rows] * masks[0]
+    for h in range(1, len(masks)):
+        total = total + stacked[h * rows : (h + 1) * rows] * masks[h]
+    return total
+
+
+def attend_block(packed, width, rows, size, image, group, limit, kept, mixed):
+    masks = head_masks(size)
+    heads = len(masks)
+    at = pl.ds(pl.multiple_of(image * rows, 16), rows)
+    queries = packed[at, group * LANES : (group + 1) * LANES]
+    keys = packed[at, width + group * LANES : width + (group + 1) * LANES]
+    values = packed[at, 2 * width + group * LANES : 2 * width + (group + 1) * LANES]
+    scores = (nt(split_heads(keys, masks), queries) * size**-0.5).reshape(heads, rows, rows)
+    live = lax.broadcasted_iota(jnp.int32, (1, rows, 1), 1) < limit
+    scores = jnp.where(live, scores, -1e30)
+    raised = jnp.exp(scores - jnp.max(scores, axis=1, keepdims=True))
+    weights = raised * (1.0 / jnp.sum(raised, axis=1, keepdims=True))
+    low = weights.reshape(heads * rows, rows).astype(BF)
+    kept[image, group] = low
+    mixed[at, group * LANES : (group + 1) * LANES] = tn(low, split_heads(values, masks)).astype(BF)
+
+
+def attend_back_block(packed, width, rows, size, image, group, kept, grad_mixed, grad_packed):
+    masks = head_masks(size)
+    heads = len(masks)
+    at = pl.ds(pl.multiple_of(image * rows, 16), rows)
+    queries = packed[at, group * LANES : (group + 1) * LANES]
+    keys = packed[at, width + group * LANES : width + (group + 1) * LANES]
+    values = packed[at, 2 * width + group * LANES : 2 * width + (group + 1) * LANES]
+    grad_out = grad_mixed[at, group * LANES : (group + 1) * LANES]
+    low = kept[image, group]
+    weights = low.astype(F32)
+    both = weights * nt(split_heads(values, masks), grad_out)
+    inner = jnp.sum(both.reshape(heads, rows, rows), axis=1, keepdims=True)
+    grad_scores = both - (weights.reshape(heads, rows, rows) * inner).reshape(heads * rows, rows)
+    grad_scores = grad_scores.astype(BF)
+    grad_values = merge_heads(nn(low, grad_out), masks, rows)
+    grad_keys = merge_heads(nn(grad_scores, queries), masks, rows) * size**-0.5
+    grad_queries = tn(grad_scores, split_heads(keys, masks)) * size**-0.5
+    grad_packed[at, group * LANES : (group + 1) * LANES] = grad_queries.astype(BF)
+    grad_packed[at, width + group * LANES : width + (group + 1) * LANES] = grad_keys.astype(BF)
+    grad_packed[at, 2 * width + group * LANES : 2 * width + (group + 1) * LANES] = grad_values.astype(BF)
+
+
+def pad_images(source, target, rows):
+    images, count = source.shape[0], source.shape[1]
+    whole = count // 16 * 16
+    for image in range(images):
+        target[image * rows + whole : (image + 1) * rows, :] = jnp.zeros((rows - whole, target.shape[1]), target.dtype)
+        target[image * rows : image * rows + count, :] = source[image]
+
+
+def enc_forward_kernel(
+    rows, counts, stream, gains, qkv, out, up, down,
+    normed_one_out, inverse_one_out, packed_out, kept_out, mixed_out, normed_two_out, inverse_two_out, active_out, slope_out, encoded_out,
+    qkv_in, out_in, up_in, down_in, padded_in, middle,
+    normed_one, inverse_one, packed, kept, mixed, normed_two, inverse_two, active, slope, encoded, in_sems, out_sems,
+):
+    images = stream.shape[0]
+    total = images * rows
+    width = stream.shape[-1]
+    weights = [(qkv, qkv_in), (out, out_in), (up, up_in), (down, down_in)]
+    loads = [pltpu.make_async_copy(source, target, in_sems.at[i]) for i, (source, target) in enumerate(weights)]
+    for load in loads:
+        load.start()
+    results = [
+        (normed_one, normed_one_out), (inverse_one, inverse_one_out), (packed, packed_out), (kept, kept_out), (mixed, mixed_out),
+        (normed_two, normed_two_out), (inverse_two, inverse_two_out), (active, active_out), (slope, slope_out), (encoded, encoded_out),
+    ]
+    stores = [pltpu.make_async_copy(source, target, out_sems.at[i]) for i, (source, target) in enumerate(results)]
+    pad_images(stream, padded_in, rows)
+    norm_rows(total, padded_in, gains[0:1, :], normed_one, inverse_one)
+    loads[0].wait()
+
+    def project(tile):
+        packed[:, columns(tile)] = nn(normed_one[...], qkv_in[:, columns(tile)]).astype(BF)
+
+    each(qkv.shape[1] // TILE, project)
+    for store in stores[:3]:
+        store.start()
+
+    def mix(image):
+        for group in range(width // LANES):
+            attend_block(packed, width, rows, width // HEADS, image, group, counts[image], kept, mixed)
+
+    each(images, mix)
+    for store in stores[3:5]:
+        store.start()
+    loads[1].wait()
+
+    def add_out(tile):
+        middle[:, columns(tile)] = padded_in[:, columns(tile)].astype(F32) + nn(mixed[...], out_in[:, columns(tile)])
+
+    each(width // TILE, add_out)
+    norm_rows(total, middle, gains[1:2, :], normed_two, inverse_two)
+    loads[2].wait()
+    feed_up(normed_two, up_in, active, slope)
+    for store in stores[5:9]:
+        store.start()
+    loads[3].wait()
+
+    def add_down(tile):
+        encoded[:, columns(tile)] = (middle[:, columns(tile)] + nn(active[...], down_in[:, columns(tile)])).astype(BF)
+
+    each(width // TILE, add_down)
+    stores[9].start()
+    for store in stores:
+        store.wait()
+
+
+def feed_up(normed, up, active, slope):
+    def body(tile):
+        value, derivative = gelu_pair(nn(normed[...], up[:, columns(tile)]))
+        active[:, columns(tile)] = value.astype(BF)
+        slope[:, columns(tile)] = derivative.astype(BF)
+
+    each(up.shape[1] // TILE, body)
+
+
+def feed_back(grad_low, down, slope, grad_pre):
+    def body(tile):
+        grad = nt(grad_low[...], down[columns(tile), :]) * slope[:, columns(tile)].astype(F32)
+        grad_pre[:, columns(tile)] = grad.astype(BF)
+
+    each(down.shape[0] // TILE, body)
+
+
+def times_back(grad, matrix, result):
+    def body(tile):
+        result[:, columns(tile)] = nt(grad[...], matrix[columns(tile), :]).astype(result.dtype)
+
+    each(matrix.shape[0] // TILE, body)
+
+
+def one_hot(positions, image, limit, slots, places):
+    place = lax.broadcasted_iota(jnp.int32, (places, slots), 0)
+    slot = lax.broadcasted_iota(jnp.int32, (places, slots), 1)
+    return jnp.where((positions[image : image + 1, :slots] == place) & (slot < limit), 1.0, 0.0)
+
+
+def coords():
+    seq, dp = lax.axis_index("seq"), lax.axis_index("dp")
+    return {"s": dp // 4, "l": (dp // 2) % 2, "y": dp % 2, "x": seq // 2, "c": seq % 2}
+
+
+def partner(here, dim):
+    other = dict(here)
+    other[dim] = 1 - here[dim]
+    return (other["s"] * 4 + other["l"] * 2 + other["y"], other["x"] * 2 + other["c"])
+
+
+class Reduction:
+    def __init__(self, gathered, result, scratch):
+        self.gathered, self.result = gathered, result
+        self.steps = gathered.shape[1] // STEP
+        self.stage, self.land = scratch[0], scratch[1]
+        self.lands = [scratch[2 + 4 * f : 6 + 4 * f] for f in range(len(FLOWS))]
+        self.send_sem, self.recv_sem, self.load_sem = scratch[-3:]
+        self.here = coords()
+        self.next, self.ready, self.loading = 0, 0, False
+
+    @staticmethod
+    def scratch():
+        shapes = [pltpu.VMEM((2, 2, 2, 2, 2, 2, STEP, TILE), F32), pltpu.VMEM((SLOTS, 2, 2, 2, 2, STEP, TILE), F32)]
+        for _, rows, _ in FLOWS:
+            for k in range(1, 5):
+                shapes.append(pltpu.VMEM((SLOTS,) + (2,) * (4 - k) + (rows, TILE), F32))
+        return shapes + [pltpu.SemaphoreType.DMA((SLOTS, COPIES)), pltpu.SemaphoreType.DMA((SLOTS, COPIES)), pltpu.SemaphoreType.DMA((2,))]
+
+    def enter(self):
+        barrier = pltpu.get_barrier_semaphore()
+        for dim in "c" + DIMS:
+            pl.semaphore_signal(barrier, inc=1, device_id=partner(self.here, dim), device_id_type=MESH)
+        pl.semaphore_wait(barrier, 5)
+
+    def load(self, t):
+        rows = pl.ds(pl.multiple_of(t * STEP, 8), STEP)
+        whole = self.gathered.reshape(2, 2, 2, 2, 2, self.gathered.shape[1], TILE)
+        return pltpu.make_async_copy(whole.at[:, :, :, :, :, rows, :], self.stage.at[lax.rem(t, 2)], self.load_sem.at[lax.rem(t, 2)])
+
+    def core_copy(self, t):
+        slot = lax.rem(t, SLOTS)
+        return pltpu.make_async_remote_copy(
+            src_ref=self.stage.at[lax.rem(t, 2), :, :, :, :, 1 - self.here["c"]],
+            dst_ref=self.land.at[slot],
+            send_sem=self.send_sem.at[slot, COPIES - 1],
+            recv_sem=self.recv_sem.at[slot, COPIES - 1],
+            device_id=partner(self.here, "c"),
+            device_id_type=MESH,
+        )
+
+    def half(self, t, flow, k, kept):
+        first, rows, order = FLOWS[flow]
+        left = [dim for dim in DIMS if dim not in order[:k]]
+        side = self.here[order[k]] if kept else 1 - self.here[order[k]]
+        at = (lax.rem(t, SLOTS),) + tuple(side if dim == order[k] else slice(None) for dim in left)
+        if k == 0:
+            return self.land.at[at + (pl.ds(first, rows),)]
+        return self.lands[flow][k - 1].at[at]
+
+    def copy(self, t, flow, k):
+        slot = lax.rem(t, SLOTS)
+        return pltpu.make_async_remote_copy(
+            src_ref=self.half(t, flow, k, False),
+            dst_ref=self.lands[flow][k].at[slot],
+            send_sem=self.send_sem.at[slot, flow * 4 + k],
+            recv_sem=self.recv_sem.at[slot, flow * 4 + k],
+            device_id=partner(self.here, FLOWS[flow][2][k]),
+            device_id_type=MESH,
+        )
+
+    def advance(self, k, t):
+        slot = lax.rem(t, SLOTS)
+        if k == 1:
+            self.core_copy(t).wait()
+            self.land[slot] += self.stage[lax.rem(t, 2), :, :, :, :, self.here["c"]]
+            for flow in range(len(FLOWS)):
+                self.copy(t, flow, 0).start()
+            return
+        for flow in range(len(FLOWS)):
+            self.copy(t, flow, k - 2).wait()
+            kept = self.half(t, flow, k - 2, True)
+            if k < 5:
+                self.lands[flow][k - 2][slot] += kept[...]
+                self.copy(t, flow, k - 1).start()
+            else:
+                first, rows, _ = FLOWS[flow]
+                at = pl.ds(pl.multiple_of(t * STEP + first, 8), rows)
+                self.result[at, :] = self.lands[flow][3][slot] + kept[...]
+
+    def step(self, t, fresh):
+        @pl.when(t < fresh)
+        def _():
+            self.load(t).wait()
+            self.core_copy(t).start()
+
+        for k in range(1, 6):
+            @pl.when((t >= k) & (t < self.steps + k))
+            def _():
+                self.advance(k, t - k)
+
+        @pl.when(t + 1 < fresh)
+        def _():
+            self.load(t + 1).start()
+
+    def run(self, count, body, every=1):
+        first, fresh = self.next, self.ready // STEP
+        pumps = min(count // every, fresh - first)
+        if pumps <= 0:
+            each(count, body)
+            return
+        if not self.loading:
+            self.load(first).start()
+
+        def one(index):
+            body(index)
+
+            @pl.when((lax.rem(index, every) == every - 1) & (index < pumps * every))
+            def _():
+                self.step(first + lax.div(index, every), fresh)
+
+        each(count, one)
+        self.next = first + pumps
+        self.loading = self.next < fresh
+
+    def pump(self, count=1):
+        self.run(count, lambda index: None)
+
+    def finish(self, beside):
+        first, fresh = self.next, self.ready // STEP
+        if not self.loading and first < fresh:
+            self.load(first).start()
+
+        def one(index):
+            self.step(first + index, fresh)
+            beside(index)
+
+        each(self.steps + 5 - first, one)
+
+    def send(self, place, sems, tile, rows, count, every=0, slots=2):
+        start = self.ready
+
+        def copy(slot, at):
+            return pltpu.make_async_copy(place(slot), self.gathered.at[:, pl.ds(at, rows), :], sems.at[slot])
+
+        def body(n):
+            slot = lax.rem(n, slots)
+
+            @pl.when(n >= slots)
+            def _():
+                copy(slot, start).wait()
+
+            place(slot)[...] = tile(n).reshape(32, rows, TILE)
+            copy(slot, pl.multiple_of(start + n * rows, 8)).start()
+
+        if every:
+            self.run(count, body, every)
+        else:
+            each(count, body)
+        for n in range(max(count - slots, 0), count):
+            copy(n % slots, start).wait()
+        self.ready = start + count * rows
+
+
+def backward_kernel(
+    erows, drows,
+    counts, positions, gains, table, encoded, embed, dec_qkv, dec_out, dec_up, dec_down, cotangent,
+    enc_qkv, enc_out, enc_up, enc_down,
+    enc_normed_one, enc_inverse_one, enc_packed, enc_kept, enc_mixed, enc_normed_two, enc_inverse_two, enc_active, enc_slope,
+    result, input_grad, gathered, reduced, vector_sum,
+    padded_positions, grad_embedded, vector_part, vector_land, vector_send, vector_recv, dec_sems, enc_sems, tile_sems, *scratch,
+):
+    images, places, dwidth = cotangent.shape
+    slots, width = input_grad.shape[1:]
+    dhidden, hidden = dec_up.shape[1], enc_up.shape[1]
+    dtotal, etotal = images * drows, images * erows
+    reduction = Reduction(gathered, reduced, scratch)
+    mask_token, dec_gain_one, dec_gain_two = gains[2:3, :dwidth], gains[3:4, :dwidth], gains[4:5, :dwidth]
+    row = lax.broadcasted_iota(jnp.int32, (drows, 1), 0)
+    padded_positions[:images, :slots] = positions[...]
+    vector_part[...] = jnp.zeros_like(vector_part)
+
+    def pick_of(image):
+        place = lax.broadcasted_iota(jnp.int32, (drows, erows), 0)
+        slot = lax.broadcasted_iota(jnp.int32, (drows, erows), 1)
+        named = (padded_positions[image : image + 1, :erows] == place) & (slot < counts[image])
+        return jnp.where(named, 1.0, 0.0)
+
+    def decoder(
+        qkv, out, up, down, filled, normed_one, inverse_one, packed, kept, mixed, middle, normed_two, inverse_two, slope, wide_low, stage
+    ):
+        into_result = pltpu.make_async_copy(cotangent, result, dec_sems.at[0])
+        weights = [(dec_qkv, qkv), (dec_out, out), (dec_up, up), (dec_down, down)]
+        loads = [pltpu.make_async_copy(source, target, dec_sems.at[1 + i]) for i, (source, target) in enumerate(weights)]
+
+        def fill(table_in, encoded_in, embed_in):
+            starts = [(encoded, encoded_in), (embed, embed_in), (table, table_in)]
+            starts = [pltpu.make_async_copy(source, target, dec_sems.at[5 + i]) for i, (source, target) in enumerate(starts)]
+            for copy in starts + loads + [into_result]:
+                copy.start()
+            reduction.enter()
+            starts[0].wait()
+            starts[1].wait()
+            high, rest = mixed, wide_low
+
+            def embed_tile(tile):
+                value = nn(encoded_in[...], embed_in[:, columns(tile)])
+                top = value.astype(BF)
+                high[pl.ds(0, etotal), columns(tile)] = top
+                rest[pl.ds(0, etotal), columns(tile)] = (value - top.astype(F32)).astype(BF)
+
+            each(dwidth // TILE, embed_tile)
+            starts[2].wait()
+            for image in range(images):
+                pick = pick_of(image)
+                low_pick = pick.astype(BF)
+                at = pl.ds(image * erows, erows)
+                picked = nn(low_pick, high[at, :]) + nn(low_pick, rest[at, :])
+                covered = jnp.sum(pick, axis=1, keepdims=True) > 0.5
+                value = jnp.where(covered, picked, mask_token) + table_in[...]
+                filled[pl.ds(image * drows, drows), :] = jnp.where(row < places, value, 0.0).astype(BF)
+
+        pl.run_scoped(
+            fill, pltpu.VMEM(table.shape, F32), pltpu.VMEM(encoded.shape, BF), pltpu.VMEM(embed.shape, BF)
+        )
+        norm_rows(dtotal, filled, dec_gain_one, normed_one, inverse_one)
+        loads[0].wait()
+
+        def project(tile):
+            packed[:, columns(tile)] = nn(normed_one[...], qkv[:, columns(tile)]).astype(BF)
+
+        each(qkv.shape[1] // TILE, project)
+
+        def mix(image):
+            for group in range(dwidth // LANES):
+                attend_block(packed, dwidth, drows, dwidth // DHEADS, image, group, places, kept, mixed)
+
+        each(images, mix)
+        loads[1].wait()
+
+        def add_out(tile):
+            middle[:, columns(tile)] = filled[:, columns(tile)].astype(F32) + nn(mixed[...], out[:, columns(tile)])
+
+        each(dwidth // TILE, add_out)
+        norm_rows(dtotal, middle, dec_gain_two, normed_two, inverse_two)
+        loads[2].wait()
+        grad_low = wide_low
+        into_result.wait()
+        pad_images(result, grad_low, drows)
+        block = dwidth // 32
+
+        def place(slot):
+            return stage.at[:, pl.ds(pl.multiple_of(slot * block, 8), block), :]
+
+        def feed(active):
+            feed_up(normed_two, up, active, slope)
+            reduction.send(lambda slot: stage, tile_sems, lambda n: tn(active[...], grad_low[:, columns(n)]), dhidden // 32, dwidth // TILE, slots=1)
+            reduction.pump()
+            loads[3].wait()
+            for tile in range(dwidth // TILE):
+                at = slice(tile * TILE, (tile + 1) * TILE)
+                value = (middle[:, at] + nn(active[...], down[:, at])).astype(BF)
+                for image in range(images):
+                    result[image, :, at] = value[image * drows : image * drows + places]
+
+        pl.run_scoped(feed, pltpu.VMEM((dtotal, dhidden), BF))
+        reduction.pump()
+        feed_back(grad_low, down, slope, slope)
+        reduction.pump()
+        reduction.send(place, tile_sems, lambda n: tn(normed_two[...], slope[:, columns(n)]), block, dhidden // TILE)
+        reduction.pump()
+        times_back(slope, up, middle)
+        reduction.pump()
+        grad_attend = wide_low
+
+        def keep_middle(at, grad):
+            middle[at, :] = grad
+            grad_attend[at, :] = grad.astype(BF)
+
+        def late(wide, partial):
+            vector_part[0, 4:5, :dwidth] = norm_back(
+                dtotal, middle, normed_two, inverse_two, dec_gain_two, grad_low, keep_middle, partial
+            )
+            reduction.pump()
+            reduction.send(place, tile_sems, lambda n: tn(mixed[...], grad_attend[:, columns(n)]), block, dwidth // TILE)
+            grad_mixed = normed_two
+            times_back(grad_attend, out, grad_mixed)
+
+            def mix_back(image):
+                for group in range(dwidth // LANES):
+                    attend_back_block(packed, dwidth, drows, dwidth // DHEADS, image, group, kept, grad_mixed, packed)
+
+            reduction.run(images, mix_back, 3)
+            reduction.send(place, tile_sems, lambda n: tn(normed_one[...], packed[:, columns(n)]), block, 3 * dwidth // TILE)
+            reduction.pump()
+            times_back(packed, qkv, wide)
+
+            def keep_filled(at, grad):
+                filled[at, :] = grad.astype(BF)
+
+            vector_part[0, 3:4, :dwidth] = norm_back(
+                dtotal, wide, normed_one, inverse_one, dec_gain_one, middle, keep_filled, partial
+            )
+            reduction.pump()
+
+        pl.run_scoped(late, pltpu.VMEM((dtotal, dwidth), F32), pltpu.VMEM((8, dwidth), F32))
+        token = jnp.zeros((1, dwidth), F32)
+        for image in range(images):
+            pick = pick_of(image)
+            covered = jnp.sum(pick, axis=1, keepdims=True) > 0.5
+            grad = filled[pl.ds(image * drows, drows), :]
+            token = token + jnp.sum(jnp.where(covered | (row >= places), 0.0, grad.astype(F32)), axis=0, keepdims=True)
+            grad_embedded[pl.ds(image * erows, erows), :] = tn(pick.astype(BF), grad).astype(BF)
+        vector_part[0, 2:3, :dwidth] = token
+
+    dgroups, dheads = dwidth // LANES, DHEADS * LANES // dwidth
+    wide_shape = (dtotal, dwidth)
+    pl.run_scoped(
+        decoder,
+        *[pltpu.VMEM(ref.shape, BF) for ref in (dec_qkv, dec_out, dec_up, dec_down)],
+        pltpu.VMEM(wide_shape, BF), pltpu.VMEM(wide_shape, BF), pltpu.VMEM((dtotal, 1), F32), pltpu.VMEM((dtotal, 3 * dwidth), BF),
+        pltpu.VMEM((images, dgroups, dheads * drows, drows), BF), pltpu.VMEM(wide_shape, BF), pltpu.VMEM(wide_shape, F32),
+        pltpu.VMEM(wide_shape, BF), pltpu.VMEM((dtotal, 1), F32), pltpu.VMEM((dtotal, dhidden), BF), pltpu.VMEM(wide_shape, BF),
+        pltpu.VMEM((32, dhidden // 32, TILE), F32),
+    )
+
+    def encoder(
+        embed_in, out, weight, down, normed_one, inverse_one, packed, kept, mixed, normed_two, inverse_two, grad_pre,
+        grad_low, grad_attend, middle, wide, stage,
+    ):
+        sources = [
+            (embed, embed_in), (enc_down, down), (enc_slope, grad_pre), (enc_normed_two, normed_two), (enc_up, weight),
+            (enc_inverse_two, inverse_two), (enc_out, out), (enc_mixed, mixed), (enc_packed, packed), (enc_kept, kept),
+            (enc_normed_one, normed_one), (enc_inverse_one, inverse_one),
+        ]
+        loads = [pltpu.make_async_copy(source, target, enc_sems.at[i]) for i, (source, target) in enumerate(sources)]
+        block = width // 32
+
+        def place(slot):
+            return stage.at[:, pl.ds(pl.multiple_of(slot * block, 8), block), :]
+
+        def feed(active, encoded_in):
+            starts = [(encoded, encoded_in), (enc_active, active)]
+            starts = [pltpu.make_async_copy(source, target, enc_sems.at[len(loads) + i]) for i, (source, target) in enumerate(starts)]
+            for copy in starts + loads:
+                copy.start()
+            starts[0].wait()
+            reduction.send(place, tile_sems, lambda n: tn(encoded_in[...], grad_embedded[:, columns(n)]), block, dwidth // TILE)
+            loads[0].wait()
+            times_back(grad_embedded, embed_in, wide)
+
+            def low_chunk(chunk):
+                at = pl.ds(pl.multiple_of(chunk * CHUNK, CHUNK), CHUNK)
+                grad_low[at, :] = wide[at, :].astype(BF)
+
+            each(etotal // CHUNK, low_chunk)
+            reduction.pump()
+            starts[1].wait()
+            reduction.send(lambda slot: stage, tile_sems, lambda n: tn(active[...], grad_low[:, columns(n)]), hidden // 32, width // TILE, slots=1)
+
+        pl.run_scoped(feed, pltpu.VMEM(enc_active.shape, BF), pltpu.VMEM(encoded.shape, BF))
+        reduction.pump()
+        loads[1].wait()
+        loads[2].wait()
+        feed_back(grad_low, down, grad_pre, grad_pre)
+        reduction.pump()
+        loads[3].wait()
+        reduction.send(place, tile_sems, lambda n: tn(normed_two[...], grad_pre[:, columns(n)]), block, hidden // TILE, every=6)
+        loads[4].wait()
+        times_back(grad_pre, weight, middle)
+        reduction.pump()
+        into_qkv = pltpu.make_async_copy(enc_qkv, weight.at[:, : enc_qkv.shape[1]], enc_sems.at[len(loads) + 2])
+        into_qkv.start()
+        loads[5].wait()
+
+        def late(grad_mixed, partial, input_stage):
+            def keep_middle(at, grad):
+                middle[at, :] = grad
+                grad_attend[at, :] = grad.astype(BF)
+
+            vector_part[0, 1:2, :] = norm_back(etotal, middle, normed_two, inverse_two, gains[1:2, :], wide, keep_middle, partial)
+            loads[6].wait()
+            loads[7].wait()
+            reduction.pump()
+            reduction.send(place, tile_sems, lambda n: tn(mixed[...], grad_attend[:, columns(n)]), block, width // TILE)
+            times_back(grad_attend, out, grad_mixed)
+            for load in loads[8:]:
+                load.wait()
+
+            def mix_back(image):
+                for group in range(width // LANES):
+                    attend_back_block(packed, width, erows, width // HEADS, image, group, kept, grad_mixed, packed)
+
+            reduction.run(images, mix_back, 3)
+            reduction.send(place, tile_sems, lambda n: tn(normed_one[...], packed[:, columns(n)]), block, 3 * width // TILE, every=9)
+            left = gathered.shape[1] - reduction.ready
+            if left:
+                stage[:, :left, :] = jnp.zeros((32, left, TILE), F32)
+                rest = pltpu.make_async_copy(
+                    stage.at[:, pl.ds(0, left), :], gathered.at[:, pl.ds(reduction.ready, left), :], tile_sems.at[0]
+                )
+                rest.start()
+                rest.wait()
+                reduction.ready += left
+            into_qkv.wait()
+            times_back(packed, weight.at[:, : enc_qkv.shape[1]], wide)
+            reduction.pump()
+
+            def keep_input(at, grad):
+                wide[at, :] = grad
+
+            vector_part[0, 0:1, :] = norm_back(etotal, wide, normed_one, inverse_one, gains[0:1, :], middle, keep_input, partial)
+            for image in range(images):
+                input_stage[image] = wide[image * erows : image * erows + slots, :]
+            store = pltpu.make_async_copy(input_stage, input_grad, tile_sems.at[0])
+            store.start()
+            reduction.pump()
+            store.wait()
+
+        pl.run_scoped(
+            late, pltpu.VMEM((etotal, width), BF), pltpu.VMEM((8, width), F32), pltpu.VMEM(input_grad.shape, F32)
+        )
+
+    pl.run_scoped(
+        encoder,
+        pltpu.VMEM(embed.shape, BF), pltpu.VMEM(enc_out.shape, BF), pltpu.VMEM(enc_up.shape, BF), pltpu.VMEM(enc_down.shape, BF),
+        pltpu.VMEM(enc_normed_one.shape, BF), pltpu.VMEM(enc_inverse_one.shape, F32), pltpu.VMEM(enc_packed.shape, BF),
+        pltpu.VMEM(enc_kept.shape, BF), pltpu.VMEM(enc_mixed.shape, BF), pltpu.VMEM(enc_normed_two.shape, BF),
+        pltpu.VMEM(enc_inverse_two.shape, F32), pltpu.VMEM(enc_slope.shape, BF),
+        pltpu.VMEM((etotal, width), BF), pltpu.VMEM((etotal, width), BF), pltpu.VMEM((etotal, width), F32), pltpu.VMEM((etotal, width), F32),
+        pltpu.VMEM((32, hidden // 32, TILE), F32),
+    )
+    order = "c" + DIMS
+
+    def vector_copy(k):
+        return pltpu.make_async_remote_copy(
+            src_ref=vector_part.at[k],
+            dst_ref=vector_land.at[k],
+            send_sem=vector_send.at[k],
+            recv_sem=vector_recv.at[k],
+            device_id=partner(reduction.here, order[k]),
+            device_id_type=MESH,
+        )
+
+    def vector_step(index):
+        for k in range(6):
+            @pl.when(index == k)
+            def _():
+                if k:
+                    vector_copy(k - 1).wait()
+                    vector_part[k] = vector_part[k - 1] + vector_land[k - 1]
+                if k < 5:
+                    vector_copy(k).start()
+
+    reduction.finish(vector_step)
+    vector_sum[...] = vector_part[5]
+
+
+def unpack_kernel(source, *targets):
+    at = 0
+    for target in targets:
+        block, width = target.shape
+        for n in range(width // TILE):
+            target[:, n * TILE : (n + 1) * TILE] = source[at : at + block, :]
+            at += block
+
+
+def vmem(count):
+    return [pl.BlockSpec(memory_space=pltpu.VMEM)] * count
+
+
+def anywhere(count):
+    return [pl.BlockSpec(memory_space=pl.ANY)] * count
+
+
+def shapes(*pairs):
+    return [jax.ShapeDtypeStruct(shape, dtype) for shape, dtype in pairs]
+
+
+def scratches(*pairs):
+    return [pltpu.VMEM(shape, dtype) for shape, dtype in pairs]
+
+
+def fast_local(
+    enc_input, keep_count, keep_positions,
+    enc_gain_one, enc_qkv_weight, enc_out_weight, enc_gain_two, enc_up_weight, enc_down_weight,
+    embed_weight, mask_token,
+    dec_gain_one, dec_qkv_weight, dec_out_weight, dec_gain_two, dec_up_weight, dec_down_weight,
+    cotangent,
+):
+    images, slots, width = enc_input.shape
+    places, dwidth = cotangent.shape[1:]
+    hidden, dhidden = enc_up_weight.shape[1], dec_up_weight.shape[1]
+    erows, drows = padded(slots, 16), padded(places, 16)
+    etotal, dtotal = images * erows, images * drows
+    egroups, dgroups = width // LANES, dwidth // LANES
+    eheads, dheads = HEADS // egroups, DHEADS // dgroups
+    smem = [pl.BlockSpec(memory_space=pltpu.SMEM)]
+    settings = functools.partial(pltpu.CompilerParams, vmem_limit_bytes=VMEM_BYTES)
+    vectors = (enc_gain_one, enc_gain_two, mask_token, dec_gain_one, dec_gain_two)
+    gains = jnp.stack([jnp.pad(vector, (0, width - vector.shape[0])) for vector in vectors]).astype(F32)
+    gains = jnp.pad(gains, ((0, 8 - len(vectors)), (0, 0)))
+
+    saved = shapes(
+        ((etotal, width), BF), ((etotal, 1), F32), ((etotal, 3 * width), BF), ((images, egroups, eheads * erows, erows), BF),
+        ((etotal, width), BF), ((etotal, width), BF), ((etotal, 1), F32), ((etotal, hidden), BF), ((etotal, hidden), BF), ((etotal, width), BF),
+    )
+    normed_one, inverse_one, packed, kept, mixed, normed_two, inverse_two, active, slope, encoded = pl.pallas_call(
+        functools.partial(enc_forward_kernel, erows),
+        name="enc_forward",
+        out_shape=saved,
+        in_specs=smem + vmem(2) + anywhere(4),
+        out_specs=anywhere(10),
+        scratch_shapes=scratches(
+            *((weight.shape, BF) for weight in (enc_qkv_weight, enc_out_weight, enc_up_weight, enc_down_weight)),
+            ((etotal, width), BF), ((etotal, width), F32), *((array.shape, array.dtype) for array in saved),
+        ) + [pltpu.SemaphoreType.DMA((4,)), pltpu.SemaphoreType.DMA((10,))],
+        compiler_params=settings(),
+    )(keep_count, enc_input, gains, enc_qkv_weight, enc_out_weight, enc_up_weight, enc_down_weight)
+
+    table = jnp.asarray(position_rows(places, dwidth, drows))
+    block = dwidth // 32
+    eblock = width // 32
+    layout = (
+        (dhidden // 32, dwidth), (block, dhidden), (block, dwidth), (block, 3 * dwidth), (eblock, dwidth),
+        (hidden // 32, width), (eblock, hidden), (eblock, width), (eblock, 3 * width),
+    )
+    share_rows = padded(sum(rows * columns // TILE for rows, columns in layout), STEP)
+    dec_output, input_grad, _, reduced, vector_sum = pl.pallas_call(
+        functools.partial(backward_kernel, erows, drows),
+        name="backward",
+        out_shape=shapes(
+            (cotangent.shape, BF), (enc_input.shape, F32), ((32, share_rows, TILE), F32), ((share_rows, TILE), F32), ((8, width), F32),
+        ),
+        in_specs=smem + vmem(2) + anywhere(21),
+        out_specs=vmem(1) + anywhere(2) + vmem(2),
+        scratch_shapes=scratches(
+            ((8, LANES), jnp.int32), ((etotal, dwidth), BF), ((6, 8, width), F32), ((5, 8, width), F32),
+        ) + [pltpu.SemaphoreType.DMA((count,)) for count in (5, 5, 8, 15, 2)] + Reduction.scratch(),
+        compiler_params=settings(collective_id=0, has_side_effects=True),
+    )(
+        keep_count, keep_positions, gains, table, encoded, embed_weight, dec_qkv_weight, dec_out_weight, dec_up_weight, dec_down_weight,
+        cotangent, enc_qkv_weight, enc_out_weight, enc_up_weight, enc_down_weight,
+        normed_one, inverse_one, packed, kept, mixed, normed_two, inverse_two, active, slope,
+    )
+    dec_down, dec_up, dec_out, dec_qkv, embed, enc_down, enc_up, enc_out, enc_qkv = pl.pallas_call(
+        unpack_kernel,
+        name="unpack",
+        out_shape=shapes(*((shape, F32) for shape in layout)),
+        in_specs=vmem(1),
+        out_specs=vmem(9),
+    )(reduced)
+    index = lax.axis_index("dp") * lax.axis_size("seq") + lax.axis_index("seq")
+    cuts = []
+    for at, vector in enumerate(vectors):
+        size = vector.shape[0] // 32
+        cuts.append(lax.dynamic_slice(vector_sum, (at, index * size), (1, size))[0])
+    return (
+        dec_output, input_grad, cuts[0], enc_qkv, enc_out, cuts[1], enc_up, enc_down, embed, cuts[2],
+        cuts[3], dec_qkv, dec_out, cuts[4], dec_up, dec_down,
+    )
+
+
+def position_rows(places, width, rows):
+    side = math.isqrt(places)
+    quarter = width // 4
+    place = np.arange(places)
+    rate = 1.0 / 10000.0 ** (np.arange(quarter) / quarter)
+    across, down = place[:, None] % side * rate, place[:, None] // side * rate
+    table = np.concatenate([np.sin(across), np.cos(across), np.sin(down), np.cos(down)], axis=1)
+    return np.pad(table, ((0, rows - places), (0, 0))).astype(np.float32)
+
+
 def solution(mesh):
     placed = (
         P(("dp", "seq"), None, None),
@@ -400,8 +1194,9 @@
         P(),
         P(("dp", "seq"), None, None),
     )
+    fast = (mesh.shape["dp"], mesh.shape["seq"]) == (8, 4)
     return jax.shard_map(
-        local,
+        fast_local if fast else local,
         mesh=mesh,
         in_specs=placed,
         out_specs=(

time: 1850 us -> 308 us (0.17)
  waiting for transfers between devices: 1090 us -> 0 us
  matrix products: 541 us -> 0 us
  Pallas kernels: 0 us -> 296 us
  local copies, waits for them, and re-layouts: 82.8 us -> 9.87 us
  other arithmetic: 70.3 us -> 0.62 us
  blocking collectives: 42.2 us -> 0 us
    reduce_scatter x9 -> x0, waiting for transfers between devices: 1080 us -> none  [the longest x1 142 us: local(): lax.psum_scatter(totals[4], ('dp', 'seq'), scatter_dimension=0, tiled=True)]
    dot_general x222 -> x0, matrix products: 515 us -> none  [the longest x54 209 us: outer_sum(): lax.dot_general(flat_left, flat_right, (((0,), (0,)), ((), ())), preferre...]
    pallas_call x0 -> x3, Pallas kernels: none -> 296 us  [the longest x1 262 us: fast_local(): pl.pallas_call(functools.partial(backward_kernel, erows, drows), name='ba...]
    while x1212 -> x0, local copies, waits for them, and re-layouts: 49.8 us -> none
    unnamed x1 -> x0, blocking collectives: 42.2 us -> none
    sub x12 -> x0, matrix products: 26.2 us -> none  [attend(): raised = jnp.exp(scores - row_max)]
    reduce_sum x48 -> x0, other arithmetic: 24.7 us -> none  [the longest x24 10.3 us: layer_norm(): jnp.mean(centered * centered, axis=-1, keepdims=True) + eps]
  transfers between devices with their start and end apart: 9 -> 0, of which waited for: 9 -> 0; matrix products, arithmetic and copies ran while one was open for 0% -> 0% of each run, Pallas kernels for 0% -> 0%
where the time goes in v3:
time: 308 us; the launch traced here: 307 us
  Pallas kernels  296 us (96%)
  local copies, waits for them, and re-layouts  9.87 us (3%)
    pallas_call x1, Pallas kernels, fast_local(): pl.pallas_call(functools.partial(backward_kernel, erows, drows), name='ba...  262 us
    pallas_call x1, Pallas kernels, fast_local(): pl.pallas_call(functools.partial(enc_forward_kernel, erows), name='enc_fo...  31.7 us

profile of v3, /device:TPU:0, one launch (start us, length us, event | category | flops | bytes accessed | tf_op | source)
XLA Modules:
  0.0 307.1 jit_solution(970062084260272389)
XLA Ops:
  0.6 0.7 pad.16
  1.3 0.7 pad.17
  2.0 0.7 pad.18
  2.7 0.7 stack.18
  3.4 0.7 stack.19
  4.1 0.6 pad_convert_fusion.gains
  4.7 31.7 %enc_forward.1 = (bf16[672,768]{1,0:T(8,128)(2,1)}, f32[672,1]{1,0:T(8,128)}, bf16[672,2304]{1,0:T(8,128)(2,1)}, bf16[6,6,224,112]{3,2,1,0:T(8,128)(2,1)}, bf16[...) custom-call(s32[6]{0:T(128)} %counts.3, ...), custom_call_target="tpu_custom_call" | custom-call | tf_op jit(solution)/shard_map/enc_forward/pallas_call | solution.py:1110
  36.5 261.7 %backward.1 = (bf16[6,196,512]{2,1,0:T(8,128)(2,1)}, f32[6,98,768]{2,1,0:T(8,128)}, f32[32,1320,256]{2,1,0:T(8,128)}, f32[1320,256]{1,0:T(8,128)}, f32[8,768]{1,0:T(8,128)}) custom-call(s32[6]{0:T(128)} %counts.3, s32[6,98]{1,0:T(8,128)} %positions.1, f32[8,768]{1,0:T(8,128)} %pad_convert_fusion.gains, f32[208,512]{1,0:T(8,128)} %constant.31.clone.table, ...), custom_call_target="tpu_custom_call" | custom-call | tf_op jit(solution)/shard_map/backward/pallas_call | solution.py:1131
  298.2 0.0 copy-start
  298.2 2.5 unpack.1
  300.7 1.4 dynamic-slice_bitcast_fusion
  302.1 1.4 dynamic-slice_bitcast_fusion.3
  303.4 2.4 copy.37
  305.8 0.0 copy-done
  305.8 1.3 copy.38
  (4 shorter events, 0.1 us)
Async XLA Ops:
  298.2 7.7 %copy-start = (f32[6,98,768]{2,1,0:T(8,128)S(1)}, f32[6,98,768]{2,1,0:T(8,128)}, u32[]{:S(2)}) copy-start(f32[6,98,768]{2,1,0:T(8,128)} %get-tuple-element.84) | copy-start | bytes 5419012
